TPU v7x, 32 devices: a whole 2x2x4 slice. The times are simulated.
32 devices in a mesh: dp: 16 (over z, y, core), sub: 2 (over x).
Axes of the slice: x: 2, y: 2, z: 4, core: 2. Of those that a mesh axis runs over, the one named last changes fastest.
Arguments:
- activations: bfloat16 [64, 14, 14, 384], P(('dp', 'sub')), may hold values from -6 to 6
- cotangent: bfloat16 [64, 14, 14, 384], P(('dp', 'sub')), may hold values from -0.29882812 to 0.29882812
- kernel: bfloat16 [384, 1152], replicated, may hold values from -0.1875 to 0.1875
- channel_gain: float32 [384], replicated, may hold values from 0.5 to 4
- master_flat: float32 [442368], P(('dp', 'sub')), may hold values from -6 to 6
- moment_mean: float32 [442368], P(('dp', 'sub')), may hold values from -2.352 to 2.352
- moment_square: float32 [442368], P(('dp', 'sub')), may hold values from 0.0025088 to 0.06272
Outputs:
- input_grad: bfloat16 [64, 14, 14, 384], P(('dp', 'sub'))
- master_next: float32 [442368], P(('dp', 'sub'))
- mean_next: float32 [442368], P(('dp', 'sub'))
- square_next: float32 [442368], P(('dp', 'sub'))
- kernel_next: bfloat16 [384, 1152], replicated
All inputs are finite; a program needn't handle non-finite values.
Results may differ from a plain program's by a relative error of at most 0.006.
Values may be sent and summed in bfloat16 or wider, within the bound.
A program may use at most 64 MiB of HBM per device.

v0:
```python
import jax
import jax.numpy as jnp
from jax import lax
from jax.sharding import PartitionSpec as P

CMID = 384
CG = 128
ADAM_STEP = 10
GROUPS = 3
FAN = 1152


HALF_ROOT = 0.7071067811865476
INV_ROOT_TAU = 0.3989422804014327


def gelu_slope(values):
    return (
        0.5 * (1.0 + lax.erf(values * HALF_ROOT))
        + values * jnp.exp(-0.5 * values * values) * INV_ROOT_TAU
    )


def forward(images, kernel_taps):
    batch, side = (images.shape[0], images.shape[1])
    padded = jnp.pad(images, ((0, 0), (1, 1), (1, 1), (0, 0))).reshape(
        batch, side + 2, side + 2, GROUPS, CG
    )
    total = jnp.zeros((batch, side, side, GROUPS, CG), jnp.float32)
    for tap_index in range(9):
        row_off, col_off = (tap_index // 3, tap_index % 3)
        window = padded[:, row_off : row_off + side, col_off : col_off + side]
        total = total + jnp.einsum(
            "bhwgc,gdc->bhwgd",
            window,
            kernel_taps[:, :, tap_index, :],
            preferred_element_type=jnp.float32,
        )
    return total.reshape(batch, side, side, GROUPS * CG)


def input_back(pre_grad, kernel_taps):
    batch, side = (pre_grad.shape[0], pre_grad.shape[1])
    padded = jnp.pad(pre_grad, ((0, 0), (1, 1), (1, 1), (0, 0))).reshape(
        batch, side + 2, side + 2, GROUPS, CG
    )
    total = jnp.zeros((batch, side, side, GROUPS, CG), jnp.float32)
    for tap_index in range(9):
        row_off, col_off = (tap_index // 3, tap_index % 3)
        window = padded[:, 2 - row_off : 2 - row_off + side, 2 - col_off : 2 - col_off + side]
        total = total + jnp.einsum(
            "bhwgd,gdc->bhwgc",
            window,
            kernel_taps[:, :, tap_index, :],
            preferred_element_type=jnp.float32,
        )
    return total.reshape(batch, side, side, GROUPS * CG)


def kernel_back(images, pre_grad):
    batch, side = (images.shape[0], images.shape[1])
    padded = jnp.pad(images, ((0, 0), (1, 1), (1, 1), (0, 0))).reshape(
        batch, side + 2, side + 2, GROUPS, CG
    )
    upstream = pre_grad.reshape(batch, side, side, GROUPS, CG)
    terms = []
    for tap_index in range(9):
        row_off, col_off = (tap_index // 3, tap_index % 3)
        window = padded[:, row_off : row_off + side, col_off : col_off + side]
        terms.append(
            jnp.einsum("bhwgc,bhwgd->gdc", window, upstream, preferred_element_type=jnp.float32)
        )
    return jnp.stack(terms, axis=2).reshape(GROUPS * CG * 9 * CG)


def channel_scale(sum_plain, sum_square, channel_gain):
    chan_mean = sum_plain / FAN
    chan_var = sum_square / FAN - chan_mean * chan_mean
    return (chan_mean, channel_gain / jnp.sqrt(FAN * chan_var + 0.0001))


def on_device(
    activations, cotangent, kernel, channel_gain, master_flat, moment_mean, moment_square
):
    kernel_taps = kernel.reshape(GROUPS, CG, 9, CG)
    preact = forward(activations, kernel_taps)
    pre_grad = (cotangent.astype(jnp.float32) * gelu_slope(preact)).astype(jnp.bfloat16)
    grad_full = kernel_back(activations, pre_grad)
    grad_shard = lax.psum_scatter(grad_full, ("dp", "sub"), scatter_dimension=0, tiled=True)
    input_grad = input_back(pre_grad, kernel_taps).astype(jnp.bfloat16)
    mean_next = 0.9 * moment_mean + 0.1 * grad_shard
    square_next = 0.999 * moment_square + 0.001 * grad_shard * grad_shard
    fix_mean = 1.0 - 0.9**ADAM_STEP
    fix_square = 1.0 - 0.999**ADAM_STEP
    update = mean_next / fix_mean / (jnp.sqrt(square_next / fix_square) + 1e-08)
    master_next = master_flat - 0.02 * update
    shard_len = master_next.shape[0]
    shard_start = lax.axis_index(("dp", "sub")) * shard_len
    first_chan = shard_start // FAN
    chan_span = shard_len // FAN + 2
    offsets = shard_start + jnp.arange(shard_len, dtype=jnp.int32)
    local_chan = offsets // FAN - first_chan
    onehot = (local_chan[:, None] == jnp.arange(chan_span, dtype=jnp.int32)[None, :]).astype(
        jnp.float32
    )
    highest = lax.Precision.HIGHEST
    plain_part = jnp.dot(master_next, onehot, precision=highest)
    square_part = jnp.dot(master_next * master_next, onehot, precision=highest)
    empty = jnp.zeros((CMID + chan_span,), jnp.float32)
    plain_full = lax.dynamic_update_slice(empty, plain_part, (first_chan,))[:CMID]
    square_full = lax.dynamic_update_slice(empty, square_part, (first_chan,))[:CMID]
    sum_plain, sum_square = lax.psum((plain_full, square_full), ("dp", "sub"))
    chan_mean, chan_scale = channel_scale(sum_plain, sum_square, channel_gain)
    mean_window = lax.dynamic_slice(
        jnp.concatenate([chan_mean, empty[:chan_span]]), (first_chan,), (chan_span,)
    )
    scale_window = lax.dynamic_slice(
        jnp.concatenate([chan_scale, empty[:chan_span]]), (first_chan,), (chan_span,)
    )
    entry_mean = jnp.dot(onehot, mean_window, precision=highest)
    entry_scale = jnp.dot(onehot, scale_window, precision=highest)
    standard_shard = ((master_next - entry_mean) * entry_scale).astype(jnp.bfloat16)
    kernel_next = lax.all_gather(standard_shard, ("dp", "sub"), axis=0, tiled=True).reshape(
        CMID, FAN
    )
    return (input_grad, master_next, mean_next, square_next, kernel_next)


def solution(mesh):
    placed = (
        P(("dp", "sub"), None, None, None),
        P(("dp", "sub"), None, None, None),
        P(),
        P(),
        P(("dp", "sub")),
        P(("dp", "sub")),
        P(("dp", "sub")),
    )
    return jax.shard_map(
        on_device,
        mesh=mesh,
        in_specs=placed,
        out_specs=(
            P(("dp", "sub"), None, None, None),
            P(("dp", "sub")),
            P(("dp", "sub")),
            P(("dp", "sub")),
            P(),
        ),
        check_vma=False,
    )
```

profile of v0, /device:TPU:1, one launch (start us, length us, event | category | flops | bytes accessed | tf_op | source)
XLA Modules:
  0.0 296.3 jit_solution(12931940415201104249)
XLA Ops:
  7.2 1.2 pad.10
  8.5 0.3 reshape.83
  8.7 2.0 fusion.73
  10.7 2.3 reshape.84
  13.1 1.9 fusion.71
  15.1 0.3 fusion.49
  15.4 0.3 convolution_add_fusion.15
  15.6 0.7 copy-done.6
  16.4 0.3 convolution_add_fusion.14
  16.8 0.3 convolution_add_fusion.13
  17.0 0.4 copy-done.2
  17.4 0.3 convolution_add_fusion.12
  17.7 0.3 convolution_add_fusion.11
  18.0 0.3 convolution_add_fusion.10
  18.3 0.3 convolution_add_fusion.9
  18.5 0.3 fusion
  18.8 0.4 copy.167
  19.2 0.5 reshape.49
  19.8 1.3 fusion.17
  21.4 0.3 fusion.11
  21.7 0.4 copy-done.9
  22.1 0.3 fusion.10
  22.5 0.7 copy-done.7
  23.1 0.3 fusion.9
  23.5 0.7 copy-done.5
  24.1 0.3 fusion.8
  24.5 0.7 copy-done.3
  25.1 0.3 fusion.7
  25.5 0.7 copy-done.1
  26.1 0.3 fusion.6
  26.5 0.3 fusion.5
  26.8 0.3 fusion.4
  27.1 0.3 fusion.3
  27.5 1.1 copy.188
  28.6 1.4 reshape.52
  30.0 0.3 pad.11
  30.3 0.3 reshape.85
  30.6 0.9 fusion.72
  31.6 0.2 fusion.30
  31.8 0.2 convolution_add_fusion.7
  32.1 0.4 copy-done.23
  32.5 0.2 convolution_add_fusion.6
  32.8 0.2 convolution_add_fusion.5
  33.0 0.4 copy-done.19
  33.4 0.2 convolution_add_fusion.4
  33.7 0.2 convolution_add_fusion.3
  34.0 0.4 copy-done.15
  34.4 0.2 convolution_add_fusion.2
  34.7 0.2 convolution_add_fusion.1
  35.0 0.4 copy-done.27
  35.3 0.2 fusion.2
  35.6 0.3 copy.178
  35.9 1.0 convert_element_type.23
  36.9 127.2 %all-reduce.8.cloned.1.call-done = f32[442368]{0:T(1024)} async-done(((f32[442368]{0:T(1024)}), f32[442368]{0:T(1024)}) %all-reduce.8.cloned.1.call-update) | async-done | bytes 1769488
  164.1 1.6 fusion.69
  165.7 0.7 convolution_bitcast_fusion.10
  166.4 0.7 convolution_bitcast_fusion.9
  167.3 0.2 dynamic_update_slice.7
  167.5 39.3 %all-reduce.5 = (f32[384]{0:T(512)S(1)}, f32[384]{0:T(512)S(1)}) all-reduce(f32[384]{0:T(512)S(1)} %bitcast.172, f32[384]{0:T(512)S(1)} %bitcast.173), channel_id=1, replica_groups=mesh['dp'=16,'sub'=2] {'dp','sub'}, use_global_device_ids=true, to_apply=%region_2.3 | all-reduce | flops 768 | bytes 6144 | tf_op jit(solution)/shard_map/psum | solution.py:112
  206.7 0.6 convolution_reduce_fusion.1
  207.3 0.5 convolution_reduce_fusion
  207.9 74.0 %all-gather = bf16[32,1,13824]{2,1,0:T(2,128)(2,1)S(1)} all-gather(bf16[1,1,13824]{2,1,0:T(2,128)(2,1)S(1)} %reshape.54), channel_id=1, replica_groups=mesh['dp'=16,'sub'=2] {'dp','sub'}, dimensions={0}, use_global_device_ids=true | all-gather | bytes 912384 | tf_op jit(solution)/shard_map/all_gather | solution.py:123
  281.9 5.3 %reduce.2 = bf16[32,13824]{1,0:T(8,128)(2,1)S(1)} reduce(bf16[32,1,13824]{2,1,0:T(2,128)(2,1)S(1)} %all-gather, bf16[]{:T(256)} %constant.86), dimensions={1}, to_apply=%all-gather.reduce_sub_computation | reduce | bytes 1769474 | tf_op jit(solution)/shard_map/all_gather | solution.py:123
  287.2 2.3 reshape.53
  (73 shorter events, 0.9 us)
Async XLA Ops:
  7.2 156.9 %all-reduce.8.cloned.1.call-start = ((), (), s32[]{:S(2)}) async-start(), calls=%async_computation | async-start | bytes 3538944
  10.7 6.9 %copy-start = (bf16[2,14,14,3,128]{4,3,0,2,1:T(4,128)(2,1)}, bf16[2,14,14,3,128]{4,3,0,2,1:T(4,128)(2,1)S(1)}, u32[]{:S(2)}) copy-start(bf16[2,14,14,3,128]{4,3,0,2,1:T(4,128)(2,1)S(1)} %get-tuple-element.32) | copy-start | bytes 903172
  13.1 2.0 copy-start.10
  13.1 2.3 copy-start.8
  15.0 1.7 copy-start.22
  15.0 1.7 copy-start.24
  15.0 1.7 copy-start.28
  15.0 1.7 copy-start.20
  15.0 2.0 copy-start.18
  15.0 2.6 copy-start.16
  15.0 2.9 copy-start.14
  15.1 3.2 %copy-start.12 = (bf16[3,128,1,128]{3,2,1,0:T(2,128)(2,1)}, bf16[3,128,1,128]{3,2,1,0:T(2,128)(2,1)S(1)}, u32[]{:S(2)}) copy-start(bf16[3,128,1,128]{3,2,1,0:T(2,128)(2,1)S(1)} %get-tuple-element.12) | copy-start | bytes 294916
  15.1 3.5 %copy-start.26 = (bf16[3,128,1,128]{3,2,1,0:T(2,128)(2,1)}, bf16[3,128,1,128]{3,2,1,0:T(2,128)(2,1)S(1)}, u32[]{:S(2)}) copy-start(bf16[3,128,1,128]{3,2,1,0:T(2,128)(2,1)S(1)} %get-tuple-element.11) | copy-start | bytes 294916
  15.1 1.3 copy-start.6
  15.4 1.4 copy-start.4
  16.4 1.0 copy-start.2
  18.8 1.0 copy-start.31
  19.8 1.6 copy-start.11
  21.1 1.0 copy-start.9
  22.1 1.0 copy-start.7
  23.1 1.0 copy-start.5
  24.1 1.0 copy-start.3
  25.1 1.0 copy-start.1
  30.6 1.0 copy-start.29
  30.6 1.2 copy-start.25
  31.5 0.9 copy-start.23
  31.8 1.0 copy-start.21
  32.5 0.9 copy-start.19
  32.8 0.9 copy-start.17
  33.4 0.9 copy-start.15
  33.7 1.0 copy-start.13
  34.4 0.9 copy-start.27
  34.9 129.1 %copy-start.32 = (f32[13824]{0:T(1024)S(1)}, f32[13824]{0:T(1024)}, u32[]{:S(2)}) copy-start(f32[13824]{0:T(1024)} %param.11) | copy-start | bytes 165892
  34.9 129.1 %copy-start.33 = (f32[13824]{0:T(1024)S(1)}, f32[13824]{0:T(1024)}, u32[]{:S(2)}) copy-start(f32[13824]{0:T(1024)} %param.12) | copy-start | bytes 165892
  35.0 129.1 %copy-start.34 = (f32[13824]{0:T(1024)S(1)}, f32[13824]{0:T(1024)}, u32[]{:S(2)}) copy-start(f32[13824]{0:T(1024)} %param.13) | copy-start | bytes 165892
  35.6 171.1 %copy-start.35 = (f32[384]{0:T(512)S(1)}, f32[384]{0:T(512)}, u32[]{:S(2)}) copy-start(f32[384]{0:T(512)} %param.10) | copy-start | bytes 4612
  165.6 116.3 %copy-start.30 = (f32[13824]{0:T(1024)}, f32[13824]{0:T(1024)S(1)}, u32[]{:S(2)}) copy-start(f32[13824]{0:T(1024)S(1)} %get-tuple-element.8) | copy-start | bytes 165892
Sparse Core Ops, SparseCore 0:
  30.1 133.8 all-reduce.7
where the time goes:
time: 300 us; the launch traced here: 296 us
  waiting for transfers between devices  127 us (42%)
  blocking collectives  113 us (38%)
  local copies, waits for them, and re-layouts  23 us (8%)
  between operations  14.7 us (5%)
  matrix products  9.9 us (3%)
  other arithmetic  8.3 us (3%)
    unnamed x2, waiting for transfers between devices  127 us
    all_gather x1, blocking collectives, on_device(): lax.all_gather(standard_shard, ('dp', 'sub'), axis=0, tiled=True)  74 us
    psum x1, blocking collectives, on_device(): sum_plain, sum_square = lax.psum((plain_full, square_full), ('dp', 'sub'))  39.3 us
    unnamed x73, local copies, waits for them, and re-layouts  6.1 us
  transfers between devices with their start and end apart: 1, of which 1 were waited for; matrix products, arithmetic and copies ran while one was open for 2% of the time, Pallas kernels for 0%

commit v1 on v0

--- a/solution.py
+++ b/solution.py
@@ -1,6 +1,8 @@
 import jax
 import jax.numpy as jnp
 from jax import lax
+from jax.experimental import pallas as pl
+from jax.experimental.pallas import tpu as pltpu
 from jax.sharding import PartitionSpec as P
 
 CMID = 384
@@ -126,6 +128,275 @@
     return (input_grad, master_next, mean_next, square_next, kernel_next)
 
 
+MESH = pl.DeviceIdType.MESH
+SHARD_ROWS = 12
+LINES = SHARD_ROWS * 9
+SLOT = 112
+F32 = jnp.float32
+BF16 = jnp.bfloat16
+
+
+def step_kernel(
+    act, cot, ker, gain, master, mean, square,
+    back, master_out, mean_out, square_out, ker_out,
+    pad32, cot32, xl, gl, gf, gb, r1, s1, r2, s2, r3, s3, r4, kb, kf, rows_in, rows_out,
+    rs_send, rs_recv, ag_send, ag_recv,
+):
+    dp = lax.axis_index("dp")
+    x = lax.axis_index("sub")
+    z, y, c = lax.div(dp, 4), lax.rem(lax.div(dp, 2), 2), lax.rem(dp, 2)
+    core_dev = (dp + 1 - 2 * c, x)
+    x_dev = (dp, 1 - x)
+    y_dev = (dp + 2 - 4 * y, x)
+
+    def z_dev(other):
+        return (other * 4 + lax.rem(dp, 4), x)
+
+    def ahead(k):
+        return lax.rem(z + k, 4)
+
+    def behind(k):
+        return lax.rem(z + 4 - k, 4)
+
+    barrier = pltpu.get_barrier_semaphore()
+    for device in (core_dev, x_dev, y_dev, z_dev(ahead(1)), z_dev(ahead(2)), z_dev(ahead(3))):
+        pl.semaphore_signal(barrier, inc=1, device_id=device, device_id_type=MESH)
+
+    pad32[:, :, 8:16, :] = jnp.zeros((2, 14, 8, CMID), F32)
+    cot32[:, :, 8:16, :] = jnp.zeros((2, 14, 8, CMID), F32)
+    pad32[:, :, 0:14, :] = act[...].astype(F32)
+    cot32[:, :, 0:14, :] = cot[...].astype(F32)
+    for edge in (0, 15):
+        xl[:, edge] = jnp.zeros((2, 16, 9 * CG), BF16)
+        gl[:, edge] = jnp.zeros((2, 16, 9 * CG), BF16)
+    gf[3456:3472, :] = jnp.zeros((16, CG), F32)
+
+    def shifted(values, by):
+        return values if by == 0 else pltpu.roll(values, by % 448, 0)
+
+    def grid(values):
+        return values.astype(BF16).reshape(2, 14, 16, CG)
+
+    def window(ref, top, g):
+        return ref[:, top : top + 14, :, g * 384 : g * 384 + 384].reshape(448, 384)
+
+    for g in range(GROUPS):
+        chans = slice(g * CG, g * CG + CG)
+        image = pad32[:, :, :, chans].reshape(448, CG)
+        for kx in range(3):
+            at = g * 384 + kx * CG
+            xl[:, 1:15, :, at : at + CG] = grid(shifted(image, 1 - kx))
+        preact = jnp.zeros((448, CG), F32)
+        for ky in range(3):
+            preact += lax.dot_general(
+                window(xl, ky, g), ker[chans, ky * 384 : ky * 384 + 384],
+                (((1,), (1,)), ((), ())), preferred_element_type=F32,
+            )
+        rounded = (cot32[:, :, :, chans].reshape(448, CG) * gelu_slope(preact)).astype(BF16)
+        wide = rounded.astype(F32)
+        for kx in range(3):
+            at = g * 384 + kx * CG
+            gl[:, 1:15, :, at : at + CG] = grid(shifted(wide, kx - 1))
+        turned = wide.T.astype(BF16)
+        for ky in range(3):
+            part = jnp.dot(turned, window(xl, ky, g), preferred_element_type=F32)
+            for kx in range(3):
+                line = g * 9 * CG + ky * 3 + kx
+                gf[pl.ds(line, CG, stride=9), :] = part[:, kx * CG : kx * CG + CG]
+
+    for zc in range(4):
+        for yc in range(2):
+            for cc in range(2):
+                for xc in range(2):
+                    first = (((zc * 2 + yc) * 2 + cc) * 2 + xc) * LINES
+                    gb[zc, cc, yc, xc] = gf[first : first + SLOT, :].astype(BF16)
+
+    def input_back_group(g):
+        chans = slice(g * CG, g * CG + CG)
+        total = jnp.zeros((448, CG), F32)
+        for ky in range(3):
+            taps = [ker[chans, (ky * 3 + kx) * CG : (ky * 3 + kx) * CG + CG] for kx in range(3)]
+            total += jnp.dot(
+                window(gl, 2 - ky, g), jnp.concatenate(taps, axis=0), preferred_element_type=F32
+            )
+        back[:, :, :, chans] = total.reshape(2, 14, 16, CG)[:, :, 0:14, :].astype(BF16)
+
+    def send(src, dst, send_sem, recv_sem, device):
+        copy = pltpu.make_async_remote_copy(
+            src_ref=src, dst_ref=dst, send_sem=send_sem, recv_sem=recv_sem,
+            device_id=device, device_id_type=MESH,
+        )
+        copy.start()
+        return copy
+
+    def both(one, other):
+        return one.astype(F32) + other.astype(F32)
+
+    pl.semaphore_wait(barrier, 6)
+    order = (2, 1, 3, 0)
+    copies = {}
+    for k in order:
+        copies[1, k] = send(
+            gb.at[ahead(k), 1 - c], r1.at[k], rs_send.at[0, k], rs_recv.at[0, k], core_dev
+        )
+    input_back_group(0)
+    for k in order:
+        copies[1, k].wait_recv()
+        zc = ahead(k)
+        for yc in range(2):
+            for xc in range(2):
+                one, two = (xc, yc) if k % 2 == 0 else (yc, xc)
+                s1[k, one, two] = both(gb[zc, c, yc, xc], r1[k, yc, xc]).astype(BF16)
+        mine, device = (x, x_dev) if k % 2 == 0 else (y, y_dev)
+        copies[2, k] = send(
+            s1.at[k, 1 - mine], r2.at[k], rs_send.at[1, k], rs_recv.at[1, k], device
+        )
+    input_back_group(1)
+    for k in order:
+        copies[2, k].wait_recv()
+        one, two, device = (x, y, y_dev) if k % 2 == 0 else (y, x, x_dev)
+        for b in range(2):
+            s2[k, b] = both(s1[k, one, b], r2[k, b]).astype(BF16)
+        copies[3, k] = send(
+            s2.at[k, 1 - two], r3.at[k], rs_send.at[2, k], rs_recv.at[2, k], device
+        )
+    input_back_group(2)
+    for k in order:
+        copies[3, k].wait_recv()
+        two = y if k % 2 == 0 else x
+        if k != 0:
+            s3[k] = both(s2[k, two], r3[k]).astype(BF16)
+            copies[4, k] = send(
+                s3.at[k], r4.at[k], rs_send.at[3, k], rs_recv.at[3, k], z_dev(ahead(k))
+            )
+    grad = both(s2[0, y], r3[0])
+    for k in (1, 3, 2):
+        copies[4, k].wait_recv()
+        grad = grad + r4[k].astype(F32)
+    grad = grad[0:LINES, :]
+
+    mean_next = 0.9 * mean[...] + 0.1 * grad
+    square_next = 0.999 * square[...] + 0.001 * grad * grad
+    fix_mean = 1.0 - 0.9**ADAM_STEP
+    fix_square = 1.0 - 0.999**ADAM_STEP
+    update = mean_next / fix_mean / (jnp.sqrt(square_next / fix_square) + 1e-08)
+    master_next = master[...] - 0.02 * update
+    mean_out[...] = mean_next
+    square_out[...] = square_next
+    master_out[...] = master_next
+    rows_in[0:LINES, :] = master_next
+    taps = [rows_in[pl.ds(t, SHARD_ROWS, stride=9), :] for t in range(9)]
+    plain, squares = taps[0], taps[0] * taps[0]
+    for tap in taps[1:]:
+        plain, squares = plain + tap, squares + tap * tap
+    shape = (SHARD_ROWS, CMID)
+    first_chan = (dp * 2 + x) * SHARD_ROWS
+    own = lax.broadcasted_iota(jnp.int32, shape, 1) == (
+        lax.broadcasted_iota(jnp.int32, shape, 0) + first_chan
+    )
+    own_gain = jnp.sum(jnp.where(own, gain[...], 0.0), axis=1, keepdims=True)
+    chan_mean, chan_scale = channel_scale(
+        jnp.sum(plain, axis=1, keepdims=True), jnp.sum(squares, axis=1, keepdims=True), own_gain
+    )
+    rows_out[104:SLOT, :] = jnp.zeros((8, CG), F32)
+    for t in range(9):
+        rows_out[pl.ds(t, SHARD_ROWS, stride=9), :] = (taps[t] - chan_mean) * chan_scale
+    kb[z, c, y, x] = rows_out[...].astype(BF16)
+
+    own_slot = kb.at[z, c, y, x]
+    for k in (2, 1, 3):
+        copies[5, k] = send(
+            own_slot, own_slot, ag_send.at[0, k], ag_recv.at[0, k], z_dev(ahead(k))
+        )
+    order = (0, 1, 3, 2)
+    for k in order:
+        if k != 0:
+            copies[5, k].wait_recv()
+        slot = kb.at[behind(k), c, y, x]
+        copies[6, k] = send(
+            slot, slot, ag_send.at[1, k], ag_recv.at[1, k], x_dev if k % 2 == 0 else y_dev
+        )
+    for k in order:
+        copies[6, k].wait_recv()
+        zc = behind(k)
+        slot = kb.at[zc, c, y] if k % 2 == 0 else kb.at[zc, c, :, x]
+        copies[7, k] = send(
+            slot, slot, ag_send.at[2, k], ag_recv.at[2, k], y_dev if k % 2 == 0 else x_dev
+        )
+    for k in order:
+        copies[7, k].wait_recv()
+        slot = kb.at[behind(k), c]
+        copies[8, k] = send(slot, slot, ag_send.at[3, k], ag_recv.at[3, k], core_dev)
+    for k in order:
+        copies[8, k].wait_recv()
+        zc = behind(k)
+        for yc in range(2):
+            for cc in range(2):
+                for xc in range(2):
+                    first = ((yc * 2 + cc) * 2 + xc) * LINES
+                    kf[first : first + LINES, :] = kb[zc, cc, yc, xc].astype(F32)[0:LINES, :]
+        rows = pl.ds(pl.multiple_of(zc * 96, 96), 96)
+        for t in range(9):
+            ker_out[rows, t * CG : t * CG + CG] = kf[pl.ds(t, 96, stride=9), :].astype(BF16)
+    for copy in copies.values():
+        copy.wait_send()
+
+
+def fused_on_device(
+    activations, cotangent, kernel, channel_gain, master_flat, moment_mean, moment_square
+):
+    vmem = pl.BlockSpec(memory_space=pltpu.VMEM)
+    lines = jax.ShapeDtypeStruct((LINES, CG), F32)
+    back, master_next, mean_next, square_next, kernel_next = pl.pallas_call(
+        step_kernel,
+        out_shape=(
+            jax.ShapeDtypeStruct(activations.shape, BF16),
+            lines,
+            lines,
+            lines,
+            jax.ShapeDtypeStruct((CMID, FAN), BF16),
+        ),
+        in_specs=[vmem] * 7,
+        out_specs=(vmem,) * 5,
+        scratch_shapes=[
+            pltpu.VMEM((2, 14, 16, CMID), F32),
+            pltpu.VMEM((2, 14, 16, CMID), F32),
+            pltpu.VMEM((2, 16, 16, 9 * CG), BF16),
+            pltpu.VMEM((2, 16, 16, 9 * CG), BF16),
+            pltpu.VMEM((3472, CG), F32),
+            pltpu.VMEM((4, 2, 2, 2, SLOT, CG), BF16),
+            pltpu.VMEM((4, 2, 2, SLOT, CG), BF16),
+            pltpu.VMEM((4, 2, 2, SLOT, CG), BF16),
+            pltpu.VMEM((4, 2, SLOT, CG), BF16),
+            pltpu.VMEM((4, 2, SLOT, CG), BF16),
+            pltpu.VMEM((4, SLOT, CG), BF16),
+            pltpu.VMEM((4, SLOT, CG), BF16),
+            pltpu.VMEM((4, SLOT, CG), BF16),
+            pltpu.VMEM((4, 2, 2, 2, SLOT, CG), BF16),
+            pltpu.VMEM((96 * 9, CG), F32),
+            pltpu.VMEM((SLOT, CG), F32),
+            pltpu.VMEM((SLOT, CG), F32),
+            pltpu.SemaphoreType.DMA((4, 4)),
+            pltpu.SemaphoreType.DMA((4, 4)),
+            pltpu.SemaphoreType.DMA((4, 4)),
+            pltpu.SemaphoreType.DMA((4, 4)),
+        ],
+        compiler_params=pltpu.CompilerParams(
+            collective_id=0, has_side_effects=True, vmem_limit_bytes=40 * 1024 * 1024
+        ),
+        cost_estimate=pl.CostEstimate(
+            flops=1_100_000_000, bytes_accessed=4_000_000, transcendentals=400_000
+        ),
+    )(
+        activations, cotangent, kernel, channel_gain.reshape(1, CMID),
+        master_flat.reshape(LINES, CG), moment_mean.reshape(LINES, CG),
+        moment_square.reshape(LINES, CG),
+    )
+    return (
+        back, master_next.reshape(-1), mean_next.reshape(-1), square_next.reshape(-1), kernel_next
+    )
+
+
 def solution(mesh):
     placed = (
         P(("dp", "sub"), None, None, None),
@@ -136,8 +407,9 @@
         P(("dp", "sub")),
         P(("dp", "sub")),
     )
+    fused = dict(mesh.shape) == {"dp": 16, "sub": 2}
     return jax.shard_map(
-        on_device,
+        fused_on_device if fused else on_device,
         mesh=mesh,
         in_specs=placed,
         out_specs=(

time: 300 us -> 38 us (0.13); the launches traced: 296 us -> 37.8 us
  waiting for transfers between devices: 127 us -> 0 us
  blocking collectives: 113 us -> 0 us
  Pallas kernels: 0 us -> 30.5 us
  local copies, waits for them, and re-layouts: 23 us -> 6.59 us
  between operations: 14.7 us -> 0.71 us
  matrix products: 9.9 us -> 0 us
  other arithmetic: 8.3 us -> 0 us
    unnamed x2 -> x0, waiting for transfers between devices: 127 us -> none
    all_gather x1 -> x0, blocking collectives: 74 us -> none  [on_device(): lax.all_gather(standard_shard, ('dp', 'sub'), axis=0, tiled=True)]
    psum x1 -> x0, blocking collectives: 39.3 us -> none  [on_device(): sum_plain, sum_square = lax.psum((plain_full, square_full), ('dp', 'sub'))]
    pallas_call x0 -> x1, Pallas kernels: none -> 30.5 us  [fused_on_device(): pl.pallas_call(step_kernel, out_shape=(jax.ShapeDtypeStruct(activations.s...]
    dot_general x31 -> x0, matrix products: 9.9 us -> none  [the longest x9 2.98 us: kernel_back(): jnp.einsum('bhwgc,bhwgd->gdc', window, upstream, preferred_element_type=j...]
    reshape x7 -> x1, local copies, waits for them, and re-layouts: 7.28 us -> 0.76 us  [fused_on_device(): channel_gain.reshape(1, CMID)]
    all_gather x1 -> x0, other arithmetic: 5.32 us -> none  [on_device(): lax.all_gather(standard_shard, ('dp', 'sub'), axis=0, tiled=True)]
    slice x3 -> x0, local copies, waits for them, and re-layouts: 4.81 us -> none  [the longest x1 2 us: forward(): window = padded[:, row_off:row_off + side, col_off:col_off + side]]
  transfers between devices with their start and end apart: 1 -> 0, of which waited for: 1 -> 0; matrix products, arithmetic and copies ran while one was open for 2% -> 0% of each run, Pallas kernels for 0% -> 0%
where the time goes in v1:
time: 38 us; the launch traced here: 37.8 us
  Pallas kernels  30.5 us (80%)
  local copies, waits for them, and re-layouts  6.59 us (17%)
  between operations  0.71 us (2%)
    pallas_call x1, Pallas kernels, fused_on_device(): pl.pallas_call(step_kernel, out_shape=(jax.ShapeDtypeStruct(activations.s...  30.5 us
    unnamed x15, local copies, waits for them, and re-layouts  5.83 us
    reshape x1, local copies, waits for them, and re-layouts, fused_on_device(): channel_gain.reshape(1, CMID)  0.76 us

profile of v1, /device:TPU:1, one launch (start us, length us, event | category | flops | bytes accessed | tf_op | source)
XLA Modules:
  0.0 37.8 jit_solution(8848097082247462749)
XLA Ops:
  0.6 0.0 copy-start
  0.6 0.8 %reshape.31.gain = f32[1,384]{1,0:T(1,128)S(1)} reshape(f32[384]{0:T(512)} %param.10) | data formatting | bytes 3072 | tf_op jit(solution)/shard_map/reshape | solution.py:391
  1.4 1.0 %copy.12.act = bf16[2,14,14,384]{3,2,1,0:T(8,128)(2,1)S(1)} copy(bf16[2,14,14,384]{3,0,2,1:T(2,128)(2,1)} %param.7) | data formatting | bytes 602112 | tf_op args[0]
  2.4 0.0 copy-start.1
  2.4 0.0 copy-start.2
  2.4 0.0 copy-start.3
  2.5 1.1 %copy.13.cot = bf16[2,14,14,384]{3,2,1,0:T(8,128)(2,1)S(1)} copy(bf16[2,14,14,384]{3,0,2,1:T(2,128)(2,1)} %param.8) | data formatting | bytes 602112 | tf_op args[1]
  3.5 0.0 copy-done
  3.5 0.0 copy-done.1
  3.5 0.0 copy-done.2
  3.5 0.0 copy-done.3
  3.6 30.5 %shard_map.110 = (bf16[2,14,14,384]{3,2,1,0:T(8,128)(2,1)S(1)}, f32[108,128]{1,0:T(8,128)S(1)}, f32[108,128]{1,0:T(8,128)S(1)}, f32[108,128]{1,0:T(8,128)S(1)}, bf16[384,1152]{1,0:T(8,128)(2,1)S(1)}) custom-call(bf16[2,14,14,384]{3,2,1,0:T(8,128)(2,1)S(1)} %copy.12.act, bf16[2,14,14,384]{3,2,1,0:T(8,128)(2,1)S(1)} %copy.13.cot, ...), custom_call_target="tpu_custom_call" | custom-call | flops 1100000000 | bytes 4000000 | tf_op jit(solution)/shard_map/pallas_call | solution.py:350
  34.1 0.9 %copy.14 = bf16[2,14,14,384]{3,0,2,1:T(2,128)(2,1)} copy(bf16[2,14,14,384]{3,2,1,0:T(8,128)(2,1)S(1)} %get-tuple-element.15) | data formatting | bytes 602112
  35.0 0.6 %copy.19 = f32[13824]{0:T(1024)} copy(f32[13824]{0:T(1024)S(1)} %bitcast.8) | data formatting | bytes 110592
  35.6 0.6 %copy.20 = f32[13824]{0:T(1024)} copy(f32[13824]{0:T(1024)S(1)} %bitcast.7) | data formatting | bytes 110592
  36.3 0.6 %copy.21 = f32[13824]{0:T(1024)} copy(f32[13824]{0:T(1024)S(1)} %bitcast.6) | data formatting | bytes 110592
  36.9 0.9 %copy.22 = bf16[384,1152]{1,0:T(8,128)(2,1)} copy(bf16[384,1152]{1,0:T(8,128)(2,1)S(1)} %get-tuple-element.29) | data formatting | bytes 1769472
Async XLA Ops:
  0.6 2.9 %copy-start = (bf16[384,1152]{1,0:T(8,128)(2,1)S(1)}, bf16[384,1152]{1,0:T(8,128)(2,1)}, u32[]{:S(2)}) copy-start(bf16[384,1152]{1,0:T(8,128)(2,1)} %ker.1) | copy-start | bytes 2654212
  2.4 1.1 %copy-start.1 = (f32[13824]{0:T(1024)S(1)}, f32[13824]{0:T(1024)}, u32[]{:S(2)}) copy-start(f32[13824]{0:T(1024)} %param.11) | copy-start | bytes 165892
  2.4 1.1 %copy-start.2 = (f32[13824]{0:T(1024)S(1)}, f32[13824]{0:T(1024)}, u32[]{:S(2)}) copy-start(f32[13824]{0:T(1024)} %param.12) | copy-start | bytes 165892
  2.4 1.1 %copy-start.3 = (f32[13824]{0:T(1024)S(1)}, f32[13824]{0:T(1024)}, u32[]{:S(2)}) copy-start(f32[13824]{0:T(1024)} %param.13) | copy-start | bytes 165892

commit v2 on v1

--- a/solution.py
+++ b/solution.py
@@ -139,7 +139,7 @@
 def step_kernel(
     act, cot, ker, gain, master, mean, square,
     back, master_out, mean_out, square_out, ker_out,
-    pad32, cot32, xl, gl, gf, gb, r1, s1, r2, s2, r3, s3, r4, kb, kf, rows_in, rows_out,
+    pad32, cot32, xl, gl, gf, gb, r1, s1, r2, s2, r3, s3, held, r4, kb, kf, rows_in, rows_out,
     rs_send, rs_recv, ag_send, ag_recv,
 ):
     dp = lax.axis_index("dp")
@@ -180,7 +180,7 @@
     def window(ref, top, g):
         return ref[:, top : top + 14, :, g * 384 : g * 384 + 384].reshape(448, 384)
 
-    for g in range(GROUPS):
+    def gradient_group(g):
         chans = slice(g * CG, g * CG + CG)
         image = pad32[:, :, :, chans].reshape(448, CG)
         for kx in range(3):
@@ -194,22 +194,15 @@
             )
         rounded = (cot32[:, :, :, chans].reshape(448, CG) * gelu_slope(preact)).astype(BF16)
         wide = rounded.astype(F32)
-        for kx in range(3):
-            at = g * 384 + kx * CG
-            gl[:, 1:15, :, at : at + CG] = grid(shifted(wide, kx - 1))
         turned = wide.T.astype(BF16)
         for ky in range(3):
             part = jnp.dot(turned, window(xl, ky, g), preferred_element_type=F32)
             for kx in range(3):
                 line = g * 9 * CG + ky * 3 + kx
                 gf[pl.ds(line, CG, stride=9), :] = part[:, kx * CG : kx * CG + CG]
-
-    for zc in range(4):
-        for yc in range(2):
-            for cc in range(2):
-                for xc in range(2):
-                    first = (((zc * 2 + yc) * 2 + cc) * 2 + xc) * LINES
-                    gb[zc, cc, yc, xc] = gf[first : first + SLOT, :].astype(BF16)
+        for kx in range(3):
+            at = g * 384 + kx * CG
+            gl[:, 1:15, :, at : at + CG] = grid(shifted(wide, kx - 1))
 
     def input_back_group(g):
         chans = slice(g * CG, g * CG + CG)
@@ -221,58 +214,94 @@
             )
         back[:, :, :, chans] = total.reshape(2, 14, 16, CG)[:, :, 0:14, :].astype(BF16)
 
-    def send(src, dst, send_sem, recv_sem, device):
-        copy = pltpu.make_async_remote_copy(
+    def remote(src, dst, send_sem, recv_sem, device):
+        return pltpu.make_async_remote_copy(
             src_ref=src, dst_ref=dst, send_sem=send_sem, recv_sem=recv_sem,
             device_id=device, device_id_type=MESH,
         )
+
+    def send(*parts):
+        copy = remote(*parts)
         copy.start()
         return copy
 
     def both(one, other):
         return one.astype(F32) + other.astype(F32)
 
-    pl.semaphore_wait(barrier, 6)
-    order = (2, 1, 3, 0)
     copies = {}
-    for k in order:
-        copies[1, k] = send(
-            gb.at[ahead(k), 1 - c], r1.at[k], rs_send.at[0, k], rs_recv.at[0, k], core_dev
-        )
-    input_back_group(0)
-    for k in order:
-        copies[1, k].wait_recv()
-        zc = ahead(k)
+
+    def pair_stage(zc):
+        for yc in range(2):
+            for cc in range(2):
+                for xc in range(2):
+                    first = (((zc * 2 + yc) * 2 + cc) * 2 + xc) * LINES
+                    gb[zc, cc, yc, xc] = gf[first : first + SLOT, :].astype(BF16)
+        copies[1, zc] = send(
+            gb.at[zc, 1 - c], r1.at[zc], rs_send.at[0, zc], rs_recv.at[0, zc], core_dev
+        )
+
+    def first_stage(zc):
+        copies[1, zc].wait_recv()
         for yc in range(2):
             for xc in range(2):
-                one, two = (xc, yc) if k % 2 == 0 else (yc, xc)
-                s1[k, one, two] = both(gb[zc, c, yc, xc], r1[k, yc, xc]).astype(BF16)
-        mine, device = (x, x_dev) if k % 2 == 0 else (y, y_dev)
-        copies[2, k] = send(
-            s1.at[k, 1 - mine], r2.at[k], rs_send.at[1, k], rs_recv.at[1, k], device
-        )
+                one, two = (xc, yc) if zc % 2 == 0 else (yc, xc)
+                s1[zc, one, two] = both(gb[zc, c, yc, xc], r1[zc, yc, xc]).astype(BF16)
+        mine, device = (x, x_dev) if zc % 2 == 0 else (y, y_dev)
+        copies[2, zc] = send(
+            s1.at[zc, 1 - mine], r2.at[zc], rs_send.at[1, zc], rs_recv.at[1, zc], device
+        )
+
+    def second_stage(zc):
+        copies[2, zc].wait_recv()
+        one, two, device = (x, y, y_dev) if zc % 2 == 0 else (y, x, x_dev)
+        for b in range(2):
+            s2[zc, b] = both(s1[zc, one, b], r2[zc, b]).astype(BF16)
+        copies[3, zc] = send(
+            s2.at[zc, 1 - two], r3.at[zc], rs_send.at[2, zc], rs_recv.at[2, zc], device
+        )
+
+    def line_copy(src_z, dst_z):
+        return remote(
+            s3.at[dst_z], r4.at[src_z], rs_send.at[3, dst_z], rs_recv.at[3, src_z], z_dev(dst_z)
+        )
+
+    def line_stage(zc):
+        copies[3, zc].wait_recv()
+        two = y if zc % 2 == 0 else x
+        total = both(s2[zc, two], r3[zc])
+        held[zc] = total
+        s3[zc] = total.astype(BF16)
+
+        @pl.when(z != zc)
+        def _():
+            line_copy(z, zc).start()
+
+    gradient_group(0)
+    pl.semaphore_wait(barrier, 6)
+    pair_stage(0)
+    gradient_group(1)
+    pair_stage(1)
+    first_stage(0)
+    gradient_group(2)
+    pair_stage(2)
+    pair_stage(3)
+    first_stage(1)
+    second_stage(0)
+    first_stage(2)
+    first_stage(3)
+    input_back_group(0)
+    second_stage(1)
+    line_stage(0)
+    second_stage(2)
+    second_stage(3)
     input_back_group(1)
-    for k in order:
-        copies[2, k].wait_recv()
-        one, two, device = (x, y, y_dev) if k % 2 == 0 else (y, x, x_dev)
-        for b in range(2):
-            s2[k, b] = both(s1[k, one, b], r2[k, b]).astype(BF16)
-        copies[3, k] = send(
-            s2.at[k, 1 - two], r3.at[k], rs_send.at[2, k], rs_recv.at[2, k], device
-        )
-    input_back_group(2)
-    for k in order:
-        copies[3, k].wait_recv()
-        two = y if k % 2 == 0 else x
-        if k != 0:
-            s3[k] = both(s2[k, two], r3[k]).astype(BF16)
-            copies[4, k] = send(
-                s3.at[k], r4.at[k], rs_send.at[3, k], rs_recv.at[3, k], z_dev(ahead(k))
-            )
-    grad = both(s2[0, y], r3[0])
+    line_stage(1)
+    line_stage(2)
+    line_stage(3)
+    grad = held[z]
     for k in (1, 3, 2):
-        copies[4, k].wait_recv()
-        grad = grad + r4[k].astype(F32)
+        line_copy(ahead(k), ahead(k)).wait_recv()
+        grad = grad + r4[ahead(k)].astype(F32)
     grad = grad[0:LINES, :]
 
     mean_next = 0.9 * mean[...] + 0.1 * grad
@@ -289,12 +318,14 @@
     plain, squares = taps[0], taps[0] * taps[0]
     for tap in taps[1:]:
         plain, squares = plain + tap, squares + tap * tap
-    shape = (SHARD_ROWS, CMID)
+    shape = (SHARD_ROWS, CG)
     first_chan = (dp * 2 + x) * SHARD_ROWS
-    own = lax.broadcasted_iota(jnp.int32, shape, 1) == (
-        lax.broadcasted_iota(jnp.int32, shape, 0) + first_chan
-    )
-    own_gain = jnp.sum(jnp.where(own, gain[...], 0.0), axis=1, keepdims=True)
+    chan = lax.broadcasted_iota(jnp.int32, shape, 0) + first_chan
+    lane = lax.broadcasted_iota(jnp.int32, shape, 1)
+    picked = jnp.zeros(shape, F32)
+    for g in range(GROUPS):
+        picked += jnp.where(lane + g * CG == chan, gain[g : g + 1, :], 0.0)
+    own_gain = jnp.sum(picked, axis=1, keepdims=True)
     chan_mean, chan_scale = channel_scale(
         jnp.sum(plain, axis=1, keepdims=True), jnp.sum(squares, axis=1, keepdims=True), own_gain
     )
@@ -308,6 +339,7 @@
         copies[5, k] = send(
             own_slot, own_slot, ag_send.at[0, k], ag_recv.at[0, k], z_dev(ahead(k))
         )
+    input_back_group(2)
     order = (0, 1, 3, 2)
     for k in order:
         if k != 0:
@@ -340,6 +372,31 @@
             ker_out[rows, t * CG : t * CG + CG] = kf[pl.ds(t, 96, stride=9), :].astype(BF16)
     for copy in copies.values():
         copy.wait_send()
+    for k in range(1, 4):
+        line_copy(z, ahead(k)).wait_send()
+
+
+def copy_kernel(*refs):
+    count = (len(refs) - 1) // 2
+    sems = refs[-1]
+    copies = [
+        pltpu.make_async_copy(refs[i], refs[count + i], sems.at[i]) for i in range(count)
+    ]
+    for copy in copies:
+        copy.start()
+    for copy in copies:
+        copy.wait()
+
+
+def put_out(*results):
+    place = pl.BlockSpec(memory_space=pl.ANY)
+    return pl.pallas_call(
+        copy_kernel,
+        out_shape=tuple(jax.ShapeDtypeStruct(r.shape, r.dtype) for r in results),
+        in_specs=[place] * len(results),
+        out_specs=(place,) * len(results),
+        scratch_shapes=[pltpu.SemaphoreType.DMA((len(results),))],
+    )(*results)
 
 
 def fused_on_device(
@@ -371,6 +428,7 @@
             pltpu.VMEM((4, 2, SLOT, CG), BF16),
             pltpu.VMEM((4, SLOT, CG), BF16),
             pltpu.VMEM((4, SLOT, CG), BF16),
+            pltpu.VMEM((4, SLOT, CG), F32),
             pltpu.VMEM((4, SLOT, CG), BF16),
             pltpu.VMEM((4, 2, 2, 2, SLOT, CG), BF16),
             pltpu.VMEM((96 * 9, CG), F32),
@@ -388,9 +446,12 @@
             flops=1_100_000_000, bytes_accessed=4_000_000, transcendentals=400_000
         ),
     )(
-        activations, cotangent, kernel, channel_gain.reshape(1, CMID),
+        activations, cotangent, kernel, channel_gain.reshape(GROUPS, CG),
         master_flat.reshape(LINES, CG), moment_mean.reshape(LINES, CG),
         moment_square.reshape(LINES, CG),
+    )
+    master_next, mean_next, square_next, kernel_next = put_out(
+        master_next, mean_next, square_next, kernel_next
     )
     return (
         back, master_next.reshape(-1), mean_next.reshape(-1), square_next.reshape(-1), kernel_next

time: 38 us -> 73.3 us (1.93)
  Pallas kernels: 30.5 us -> 66.6 us
    pallas_call x0 -> x1, Pallas kernels: none -> 33 us  [put_out(): pl.pallas_call(copy_kernel, out_shape=tuple((jax.ShapeDtypeStruct(r.shape...]
    pallas_call x1, Pallas kernels: 30.5 us -> 33.6 us  [fused_on_device(): pl.pallas_call(step_kernel, out_shape=(jax.ShapeDtypeStruct(activations.s...]
    reshape x1 -> x0, local copies, waits for them, and re-layouts: 0.76 us -> none  [fused_on_device(): channel_gain.reshape(1, CMID)]
    unnamed x15 -> x21, local copies, waits for them, and re-layouts: 5.83 us -> 5.89 us
where the time goes in v2:
time: 73.3 us; the launch traced here: 73.2 us
  Pallas kernels  66.6 us (91%)
  local copies, waits for them, and re-layouts  5.89 us (8%)
  between operations  0.74 us (1%)
    pallas_call x1, Pallas kernels, fused_on_device(): pl.pallas_call(step_kernel, out_shape=(jax.ShapeDtypeStruct(activations.s...  33.6 us
    pallas_call x1, Pallas kernels, put_out(): pl.pallas_call(copy_kernel, out_shape=tuple((jax.ShapeDtypeStruct(r.shape...  33 us
    unnamed x21, local copies, waits for them, and re-layouts  5.89 us

profile of v2, /device:TPU:1, one launch (start us, length us, event | category | flops | bytes accessed | tf_op | source)
XLA Modules:
  0.0 73.2 jit_solution(4667070102414514435)
XLA Ops:
  0.6 0.0 copy-start.4
  0.6 1.1 %copy.12.act = bf16[2,14,14,384]{3,2,1,0:T(8,128)(2,1)S(1)} copy(bf16[2,14,14,384]{3,0,2,1:T(2,128)(2,1)} %param.7) | data formatting | bytes 602112 | tf_op args[0]
  1.7 0.0 copy-start.5
  1.7 0.0 copy-start.6
  1.8 0.0 copy-start.7
  1.8 0.0 copy-start.8
  1.8 1.0 %copy.13.cot = bf16[2,14,14,384]{3,2,1,0:T(8,128)(2,1)S(1)} copy(bf16[2,14,14,384]{3,0,2,1:T(2,128)(2,1)} %param.8) | data formatting | bytes 602112 | tf_op args[1]
  2.8 0.0 copy-done.4
  2.8 0.0 copy-done.5
  2.8 0.0 copy-done.6
  2.8 0.0 copy-done.7
  2.9 0.0 copy-done.8
  2.9 33.6 %shard_map.110 = (bf16[2,14,14,384]{3,2,1,0:T(8,128)(2,1)S(1)}, f32[108,128]{1,0:T(8,128)S(1)}, f32[108,128]{1,0:T(8,128)S(1)}, f32[108,128]{1,0:T(8,128)S(1)}, bf16[384,1152]{1,0:T(8,128)(2,1)S(1)}) custom-call(bf16[2,14,14,384]{3,2,1,0:T(8,128)(2,1)S(1)} %copy.12.act, bf16[2,14,14,384]{3,2,1,0:T(8,128)(2,1)S(1)} %copy.13.cot, ...), custom_call_target="tpu_custom_call" | custom-call | flops 1100000000 | bytes 4000000 | tf_op jit(solution)/shard_map/pallas_call | solution.py:407
  36.5 0.0 copy-start
  36.5 0.9 %copy-done = bf16[384,1152]{1,0:T(8,128)(2,1)} copy-done((bf16[384,1152]{1,0:T(8,128)(2,1)}, bf16[384,1152]{1,0:T(8,128)(2,1)S(1)}, u32[]{:S(2)}) %copy-start) | copy-done | bytes 884760
  37.4 0.0 copy-start.1
  37.4 0.6 copy-done.1
  38.0 0.0 copy-start.2
  38.0 0.6 copy-done.2
  38.6 0.0 copy-start.3
  38.6 0.6 copy-done.3
  39.3 0.9 %copy.14 = bf16[2,14,14,384]{3,0,2,1:T(2,128)(2,1)} copy(bf16[2,14,14,384]{3,2,1,0:T(8,128)(2,1)S(1)} %get-tuple-element.23) | data formatting | bytes 602112
  40.2 33.0 %shard_map.111 = (f32[108,128]{1,0:T(8,128)}, f32[108,128]{1,0:T(8,128)}, f32[108,128]{1,0:T(8,128)}, bf16[384,1152]{1,0:T(8,128)(2,1)}) custom-call(f32[108,128]{1,0:T(8,128)} %copy-done.1, f32[108,128]{1,0:T(8,128)} %copy-done.2, f32[108,128]{1,0:T(8,128)} %copy-done.3, bf16[384,1152]{1,0:T(8,128)(2,1)} %copy-done), custom_call_target="tpu_custom_call" | custom-call | tf_op jit(solution)/shard_map/pallas_call | solution.py:393
Async XLA Ops:
  0.6 2.2 %copy-start.4 = (bf16[384,1152]{1,0:T(8,128)(2,1)S(1)}, bf16[384,1152]{1,0:T(8,128)(2,1)}, u32[]{:S(2)}) copy-start(bf16[384,1152]{1,0:T(8,128)(2,1)} %ker.1) | copy-start | bytes 2654212
  1.7 1.1 %copy-start.5 = (f32[13824]{0:T(1024)S(1)}, f32[13824]{0:T(1024)}, u32[]{:S(2)}) copy-start(f32[13824]{0:T(1024)} %param.11) | copy-start | bytes 165892
  1.7 1.1 %copy-start.6 = (f32[13824]{0:T(1024)S(1)}, f32[13824]{0:T(1024)}, u32[]{:S(2)}) copy-start(f32[13824]{0:T(1024)} %param.12) | copy-start | bytes 165892
  1.8 1.1 %copy-start.7 = (f32[13824]{0:T(1024)S(1)}, f32[13824]{0:T(1024)}, u32[]{:S(2)}) copy-start(f32[13824]{0:T(1024)} %param.13) | copy-start | bytes 165892
  1.8 1.1 %copy-start.8 = (f32[384]{0:T(512)S(1)}, f32[384]{0:T(512)}, u32[]{:S(2)}) copy-start(f32[384]{0:T(512)} %param.10) | copy-start | bytes 4612
  36.5 0.9 %copy-start = (bf16[384,1152]{1,0:T(8,128)(2,1)}, bf16[384,1152]{1,0:T(8,128)(2,1)S(1)}, u32[]{:S(2)}) copy-start(bf16[384,1152]{1,0:T(8,128)(2,1)S(1)} %get-tuple-element.18.refs_3_) | copy-start | bytes 2654212
  37.4 0.6 copy-start.1
  38.0 0.6 copy-start.2
  38.6 0.6 copy-start.3

commit v3 on v2

--- a/solution.py
+++ b/solution.py
@@ -81,6 +81,15 @@
     return (chan_mean, channel_gain / jnp.sqrt(FAN * chan_var + 0.0001))
 
 
+def adam(grad, master, mean, square):
+    mean_next = 0.9 * mean + 0.1 * grad
+    square_next = 0.999 * square + 0.001 * grad * grad
+    fix_mean = 1.0 - 0.9**ADAM_STEP
+    fix_square = 1.0 - 0.999**ADAM_STEP
+    update = mean_next / fix_mean / (jnp.sqrt(square_next / fix_square) + 1e-08)
+    return (master - 0.02 * update, mean_next, square_next)
+
+
 def on_device(
     activations, cotangent, kernel, channel_gain, master_flat, moment_mean, moment_square
 ):
@@ -90,12 +99,9 @@
     grad_full = kernel_back(activations, pre_grad)
     grad_shard = lax.psum_scatter(grad_full, ("dp", "sub"), scatter_dimension=0, tiled=True)
     input_grad = input_back(pre_grad, kernel_taps).astype(jnp.bfloat16)
-    mean_next = 0.9 * moment_mean + 0.1 * grad_shard
-    square_next = 0.999 * moment_square + 0.001 * grad_shard * grad_shard
-    fix_mean = 1.0 - 0.9**ADAM_STEP
-    fix_square = 1.0 - 0.999**ADAM_STEP
-    update = mean_next / fix_mean / (jnp.sqrt(square_next / fix_square) + 1e-08)
-    master_next = master_flat - 0.02 * update
+    master_next, mean_next, square_next = adam(
+        grad_shard, master_flat, moment_mean, moment_square
+    )
     shard_len = master_next.shape[0]
     shard_start = lax.axis_index(("dp", "sub")) * shard_len
     first_chan = shard_start // FAN
@@ -138,8 +144,8 @@
 
 def step_kernel(
     act, cot, ker, gain, master, mean, square,
-    back, master_out, mean_out, square_out, ker_out,
-    pad32, cot32, xl, gl, gf, gb, r1, s1, r2, s2, r3, s3, held, r4, kb, kf, rows_in, rows_out,
+    back, grad_out, ker_out,
+    pad32, cot32, xl, gl, gf, gb, r1, s1, r2, s3, r4, kb, kf, rows_in, rows_out,
     rs_send, rs_recv, ag_send, ag_recv,
 ):
     dp = lax.axis_index("dp")
@@ -148,6 +154,7 @@
     core_dev = (dp + 1 - 2 * c, x)
     x_dev = (dp, 1 - x)
     y_dev = (dp + 2 - 4 * y, x)
+    cross_dev = (dp + 2 - 4 * y, 1 - x)
 
     def z_dev(other):
         return (other * 4 + lax.rem(dp, 4), x)
@@ -159,40 +166,41 @@
         return lax.rem(z + 4 - k, 4)
 
     barrier = pltpu.get_barrier_semaphore()
-    for device in (core_dev, x_dev, y_dev, z_dev(ahead(1)), z_dev(ahead(2)), z_dev(ahead(3))):
+    plane = (x_dev, y_dev, cross_dev)
+    line = tuple(z_dev(ahead(k)) for k in (1, 2, 3))
+    for device in (core_dev, *plane, *line):
         pl.semaphore_signal(barrier, inc=1, device_id=device, device_id_type=MESH)
 
-    pad32[:, :, 8:16, :] = jnp.zeros((2, 14, 8, CMID), F32)
-    cot32[:, :, 8:16, :] = jnp.zeros((2, 14, 8, CMID), F32)
-    pad32[:, :, 0:14, :] = act[...].astype(F32)
-    cot32[:, :, 0:14, :] = cot[...].astype(F32)
+    for wide_ref, narrow in ((pad32, act), (cot32, cot)):
+        wide_ref[:, 24:32, :] = jnp.zeros((14, 8, CMID), F32)
+        wide_ref[:, 0:28, :] = narrow[...].astype(F32)
     for edge in (0, 15):
-        xl[:, edge] = jnp.zeros((2, 16, 9 * CG), BF16)
-        gl[:, edge] = jnp.zeros((2, 16, 9 * CG), BF16)
+        xl[edge] = jnp.zeros((32, 9 * CG), BF16)
+        gl[edge] = jnp.zeros((32, 9 * CG), BF16)
     gf[3456:3472, :] = jnp.zeros((16, CG), F32)
 
     def shifted(values, by):
-        return values if by == 0 else pltpu.roll(values, by % 448, 0)
+        return values if by == 0 else pltpu.roll(values, (2 * by) % 448, 0)
 
     def grid(values):
-        return values.astype(BF16).reshape(2, 14, 16, CG)
+        return values.astype(BF16).reshape(14, 32, CG)
 
     def window(ref, top, g):
-        return ref[:, top : top + 14, :, g * 384 : g * 384 + 384].reshape(448, 384)
+        return ref[top : top + 14, :, g * 384 : g * 384 + 384].reshape(448, 384)
 
     def gradient_group(g):
         chans = slice(g * CG, g * CG + CG)
-        image = pad32[:, :, :, chans].reshape(448, CG)
+        image = pad32[:, :, chans].reshape(448, CG)
         for kx in range(3):
             at = g * 384 + kx * CG
-            xl[:, 1:15, :, at : at + CG] = grid(shifted(image, 1 - kx))
+            xl[1:15, :, at : at + CG] = grid(shifted(image, 1 - kx))
         preact = jnp.zeros((448, CG), F32)
         for ky in range(3):
             preact += lax.dot_general(
                 window(xl, ky, g), ker[chans, ky * 384 : ky * 384 + 384],
                 (((1,), (1,)), ((), ())), preferred_element_type=F32,
             )
-        rounded = (cot32[:, :, :, chans].reshape(448, CG) * gelu_slope(preact)).astype(BF16)
+        rounded = (cot32[:, :, chans].reshape(448, CG) * gelu_slope(preact)).astype(BF16)
         wide = rounded.astype(F32)
         turned = wide.T.astype(BF16)
         for ky in range(3):
@@ -202,7 +210,7 @@
                 gf[pl.ds(line, CG, stride=9), :] = part[:, kx * CG : kx * CG + CG]
         for kx in range(3):
             at = g * 384 + kx * CG
-            gl[:, 1:15, :, at : at + CG] = grid(shifted(wide, kx - 1))
+            gl[1:15, :, at : at + CG] = grid(shifted(wide, kx - 1))
 
     def input_back_group(g):
         chans = slice(g * CG, g * CG + CG)
@@ -212,7 +220,7 @@
             total += jnp.dot(
                 window(gl, 2 - ky, g), jnp.concatenate(taps, axis=0), preferred_element_type=F32
             )
-        back[:, :, :, chans] = total.reshape(2, 14, 16, CG)[:, :, 0:14, :].astype(BF16)
+        back[:, :, chans] = total.reshape(14, 32, CG)[:, 0:28, :].astype(BF16)
 
     def remote(src, dst, send_sem, recv_sem, device):
         return pltpu.make_async_remote_copy(
@@ -240,79 +248,54 @@
             gb.at[zc, 1 - c], r1.at[zc], rs_send.at[0, zc], rs_recv.at[0, zc], core_dev
         )
 
-    def first_stage(zc):
-        copies[1, zc].wait_recv()
+    def plane_stage(k):
+        zc = ahead(k)
+        remote(
+            gb.at[zc, 1 - c], r1.at[zc], rs_send.at[0, zc], rs_recv.at[0, zc], core_dev
+        ).wait_recv()
         for yc in range(2):
             for xc in range(2):
-                one, two = (xc, yc) if zc % 2 == 0 else (yc, xc)
-                s1[zc, one, two] = both(gb[zc, c, yc, xc], r1[zc, yc, xc]).astype(BF16)
-        mine, device = (x, x_dev) if zc % 2 == 0 else (y, y_dev)
-        copies[2, zc] = send(
-            s1.at[zc, 1 - mine], r2.at[zc], rs_send.at[1, zc], rs_recv.at[1, zc], device
-        )
-
-    def second_stage(zc):
-        copies[2, zc].wait_recv()
-        one, two, device = (x, y, y_dev) if zc % 2 == 0 else (y, x, x_dev)
-        for b in range(2):
-            s2[zc, b] = both(s1[zc, one, b], r2[zc, b]).astype(BF16)
-        copies[3, zc] = send(
-            s2.at[zc, 1 - two], r3.at[zc], rs_send.at[2, zc], rs_recv.at[2, zc], device
-        )
-
-    def line_copy(src_z, dst_z):
-        return remote(
-            s3.at[dst_z], r4.at[src_z], rs_send.at[3, dst_z], rs_recv.at[3, src_z], z_dev(dst_z)
-        )
-
-    def line_stage(zc):
-        copies[3, zc].wait_recv()
-        two = y if zc % 2 == 0 else x
-        total = both(s2[zc, two], r3[zc])
-        held[zc] = total
-        s3[zc] = total.astype(BF16)
-
-        @pl.when(z != zc)
-        def _():
-            line_copy(z, zc).start()
+                s1[k, yc, xc] = both(gb[zc, c, yc, xc], r1[zc, yc, xc]).astype(BF16)
+        parts = (s1.at[k, y, 1 - x], s1.at[k, 1 - y, x], s1.at[k, 1 - y, 1 - x])
+        for j in range(3):
+            copies[2 + j, k] = send(
+                parts[j], r2.at[k, j], rs_send.at[1 + j, k], rs_recv.at[1 + j, k], plane[j]
+            )
+
+    def plane_sum(k):
+        total = s1[k, y, x].astype(F32)
+        for j in range(3):
+            copies[2 + j, k].wait_recv()
+            total = total + r2[k, j].astype(F32)
+        return total
 
     gradient_group(0)
-    pl.semaphore_wait(barrier, 6)
+    pl.semaphore_wait(barrier, 7)
     pair_stage(0)
     gradient_group(1)
     pair_stage(1)
-    first_stage(0)
     gradient_group(2)
     pair_stage(2)
     pair_stage(3)
-    first_stage(1)
-    second_stage(0)
-    first_stage(2)
-    first_stage(3)
     input_back_group(0)
-    second_stage(1)
-    line_stage(0)
-    second_stage(2)
-    second_stage(3)
+    order = (2, 1, 3, 0)
+    for k in order:
+        plane_stage(k)
     input_back_group(1)
-    line_stage(1)
-    line_stage(2)
-    line_stage(3)
-    grad = held[z]
+    for k in order[0:3]:
+        s3[k] = plane_sum(k).astype(BF16)
+        copies[5, k] = send(
+            s3.at[k], r4.at[k], rs_send.at[4, k], rs_recv.at[4, k], line[k - 1]
+        )
+    grad = plane_sum(0)
+    input_back_group(2)
     for k in (1, 3, 2):
-        line_copy(ahead(k), ahead(k)).wait_recv()
-        grad = grad + r4[ahead(k)].astype(F32)
+        copies[5, k].wait_recv()
+        grad = grad + r4[k].astype(F32)
     grad = grad[0:LINES, :]
-
-    mean_next = 0.9 * mean[...] + 0.1 * grad
-    square_next = 0.999 * square[...] + 0.001 * grad * grad
-    fix_mean = 1.0 - 0.9**ADAM_STEP
-    fix_square = 1.0 - 0.999**ADAM_STEP
-    update = mean_next / fix_mean / (jnp.sqrt(square_next / fix_square) + 1e-08)
-    master_next = master[...] - 0.02 * update
-    mean_out[...] = mean_next
-    square_out[...] = square_next
-    master_out[...] = master_next
+    grad_out[...] = grad
+
+    master_next, _, _ = adam(grad, master[...], mean[...], square[...])
     rows_in[0:LINES, :] = master_next
     taps = [rows_in[pl.ds(t, SHARD_ROWS, stride=9), :] for t in range(9)]
     plain, squares = taps[0], taps[0] * taps[0]
@@ -334,33 +317,29 @@
         rows_out[pl.ds(t, SHARD_ROWS, stride=9), :] = (taps[t] - chan_mean) * chan_scale
     kb[z, c, y, x] = rows_out[...].astype(BF16)
 
-    own_slot = kb.at[z, c, y, x]
-    for k in (2, 1, 3):
-        copies[5, k] = send(
-            own_slot, own_slot, ag_send.at[0, k], ag_recv.at[0, k], z_dev(ahead(k))
-        )
-    input_back_group(2)
-    order = (0, 1, 3, 2)
-    for k in order:
+    def spread(k, slot, step, device):
+        copies[step, k] = send(
+            slot, slot, ag_send.at[step - 6, k], ag_recv.at[step - 6, k], device
+        )
+
+    def spread_own(k):
+        slot = kb.at[behind(k), c, y, x]
         if k != 0:
-            copies[5, k].wait_recv()
-        slot = kb.at[behind(k), c, y, x]
-        copies[6, k] = send(
-            slot, slot, ag_send.at[1, k], ag_recv.at[1, k], x_dev if k % 2 == 0 else y_dev
-        )
-    for k in order:
-        copies[6, k].wait_recv()
-        zc = behind(k)
-        slot = kb.at[zc, c, y] if k % 2 == 0 else kb.at[zc, c, :, x]
-        copies[7, k] = send(
-            slot, slot, ag_send.at[2, k], ag_recv.at[2, k], y_dev if k % 2 == 0 else x_dev
-        )
-    for k in order:
-        copies[7, k].wait_recv()
-        slot = kb.at[behind(k), c]
-        copies[8, k] = send(slot, slot, ag_send.at[3, k], ag_recv.at[3, k], core_dev)
-    for k in order:
-        copies[8, k].wait_recv()
+            copies[6, k].wait_recv()
+        for j in range(3):
+            spread(k, slot, 7 + j, plane[j])
+        spread(k, slot, 10, core_dev)
+
+    def relay(k):
+        held = kb.at[behind(k), c]
+        slots = (held.at[y, 1 - x], held.at[1 - y, x], held.at[1 - y, 1 - x])
+        for j in range(3):
+            copies[7 + j, k].wait_recv()
+            spread(k, slots[j], 11 + j, core_dev)
+
+    def finish(k):
+        for step in range(10, 14):
+            copies[step, k].wait_recv()
         zc = behind(k)
         for yc in range(2):
             for cc in range(2):
@@ -370,74 +349,63 @@
         rows = pl.ds(pl.multiple_of(zc * 96, 96), 96)
         for t in range(9):
             ker_out[rows, t * CG : t * CG + CG] = kf[pl.ds(t, 96, stride=9), :].astype(BF16)
+
+    for k in (2, 1, 3):
+        spread(k, kb.at[z, c, y, x], 6, line[k - 1])
+    spread_own(0)
+    spread_own(1)
+    relay(0)
+    spread_own(3)
+    relay(1)
+    spread_own(2)
+    relay(3)
+    finish(0)
+    relay(2)
+    finish(1)
+    finish(3)
+    finish(2)
     for copy in copies.values():
         copy.wait_send()
-    for k in range(1, 4):
-        line_copy(z, ahead(k)).wait_send()
-
-
-def copy_kernel(*refs):
-    count = (len(refs) - 1) // 2
-    sems = refs[-1]
-    copies = [
-        pltpu.make_async_copy(refs[i], refs[count + i], sems.at[i]) for i in range(count)
-    ]
-    for copy in copies:
-        copy.start()
-    for copy in copies:
-        copy.wait()
-
-
-def put_out(*results):
-    place = pl.BlockSpec(memory_space=pl.ANY)
-    return pl.pallas_call(
-        copy_kernel,
-        out_shape=tuple(jax.ShapeDtypeStruct(r.shape, r.dtype) for r in results),
-        in_specs=[place] * len(results),
-        out_specs=(place,) * len(results),
-        scratch_shapes=[pltpu.SemaphoreType.DMA((len(results),))],
-    )(*results)
 
 
 def fused_on_device(
     activations, cotangent, kernel, channel_gain, master_flat, moment_mean, moment_square
 ):
+    side = activations.shape[1]
+
+    def by_place(images):
+        return jnp.transpose(images, (1, 2, 0, 3)).reshape(side, side * 2, CMID)
+
     vmem = pl.BlockSpec(memory_space=pltpu.VMEM)
-    lines = jax.ShapeDtypeStruct((LINES, CG), F32)
-    back, master_next, mean_next, square_next, kernel_next = pl.pallas_call(
+    back, grad, kernel_next = pl.pallas_call(
         step_kernel,
         out_shape=(
-            jax.ShapeDtypeStruct(activations.shape, BF16),
-            lines,
-            lines,
-            lines,
+            jax.ShapeDtypeStruct((side, side * 2, CMID), BF16),
+            jax.ShapeDtypeStruct((LINES, CG), F32),
             jax.ShapeDtypeStruct((CMID, FAN), BF16),
         ),
         in_specs=[vmem] * 7,
-        out_specs=(vmem,) * 5,
+        out_specs=(vmem,) * 3,
         scratch_shapes=[
-            pltpu.VMEM((2, 14, 16, CMID), F32),
-            pltpu.VMEM((2, 14, 16, CMID), F32),
-            pltpu.VMEM((2, 16, 16, 9 * CG), BF16),
-            pltpu.VMEM((2, 16, 16, 9 * CG), BF16),
+            pltpu.VMEM((14, 32, CMID), F32),
+            pltpu.VMEM((14, 32, CMID), F32),
+            pltpu.VMEM((16, 32, 9 * CG), BF16),
+            pltpu.VMEM((16, 32, 9 * CG), BF16),
             pltpu.VMEM((3472, CG), F32),
             pltpu.VMEM((4, 2, 2, 2, SLOT, CG), BF16),
             pltpu.VMEM((4, 2, 2, SLOT, CG), BF16),
             pltpu.VMEM((4, 2, 2, SLOT, CG), BF16),
-            pltpu.VMEM((4, 2, SLOT, CG), BF16),
-            pltpu.VMEM((4, 2, SLOT, CG), BF16),
+            pltpu.VMEM((4, 3, SLOT, CG), BF16),
             pltpu.VMEM((4, SLOT, CG), BF16),
-            pltpu.VMEM((4, SLOT, CG), BF16),
-            pltpu.VMEM((4, SLOT, CG), F32),
             pltpu.VMEM((4, SLOT, CG), BF16),
             pltpu.VMEM((4, 2, 2, 2, SLOT, CG), BF16),
             pltpu.VMEM((96 * 9, CG), F32),
             pltpu.VMEM((SLOT, CG), F32),
             pltpu.VMEM((SLOT, CG), F32),
-            pltpu.SemaphoreType.DMA((4, 4)),
-            pltpu.SemaphoreType.DMA((4, 4)),
-            pltpu.SemaphoreType.DMA((4, 4)),
-            pltpu.SemaphoreType.DMA((4, 4)),
+            pltpu.SemaphoreType.DMA((5, 4)),
+            pltpu.SemaphoreType.DMA((5, 4)),
+            pltpu.SemaphoreType.DMA((8, 4)),
+            pltpu.SemaphoreType.DMA((8, 4)),
         ],
         compiler_params=pltpu.CompilerParams(
             collective_id=0, has_side_effects=True, vmem_limit_bytes=40 * 1024 * 1024
@@ -446,16 +414,15 @@
             flops=1_100_000_000, bytes_accessed=4_000_000, transcendentals=400_000
         ),
     )(
-        activations, cotangent, kernel, channel_gain.reshape(GROUPS, CG),
+        by_place(activations), by_place(cotangent), kernel, channel_gain.reshape(GROUPS, CG),
         master_flat.reshape(LINES, CG), moment_mean.reshape(LINES, CG),
         moment_square.reshape(LINES, CG),
     )
-    master_next, mean_next, square_next, kernel_next = put_out(
-        master_next, mean_next, square_next, kernel_next
-    )
-    return (
-        back, master_next.reshape(-1), mean_next.reshape(-1), square_next.reshape(-1), kernel_next
-    )
+    input_grad = jnp.transpose(back.reshape(side, side, 2, CMID), (2, 0, 1, 3))
+    master_next, mean_next, square_next = adam(
+        grad.reshape(-1), master_flat, moment_mean, moment_square
+    )
+    return (input_grad, master_next, mean_next, square_next, kernel_next)
 
 
 def solution(mesh):

time: 73.3 us -> 38.3 us (0.52)
  Pallas kernels: 66.6 us -> 32.7 us
  local copies, waits for them, and re-layouts: 5.89 us -> 4.1 us
    pallas_call x2 -> x1, Pallas kernels: 66.6 us -> 32.7 us  [fused_on_device(): pl.pallas_call(step_kernel, out_shape=(jax.ShapeDtypeStruct((side, side *...]
    unnamed x21 -> x11, local copies, waits for them, and re-layouts: 5.89 us -> 0.94 us
    reshape x0 -> x3, local copies, waits for them, and re-layouts: none -> 3.16 us  [the longest x2 2.26 us: by_place(): return jnp.transpose(images, (1, 2, 0, 3)).reshape(side, side * 2, CMID)]
where the time goes in v3:
time: 38.3 us; the launch traced here: 38.2 us
  Pallas kernels  32.7 us (85%)
  local copies, waits for them, and re-layouts  4.1 us (11%)
  between operations  0.73 us (2%)
  other arithmetic  0.68 us (2%)
    pallas_call x1, Pallas kernels, fused_on_device(): pl.pallas_call(step_kernel, out_shape=(jax.ShapeDtypeStruct((side, side *...  32.7 us
    reshape x2, local copies, waits for them, and re-layouts, by_place(): return jnp.transpose(images, (1, 2, 0, 3)).reshape(side, side * 2, CMID)  2.26 us
    unnamed x11, local copies, waits for them, and re-layouts  0.94 us
    reshape x1, local copies, waits for them, and re-layouts, fused_on_device(): input_grad = jnp.transpose(back.reshape(side, side, 2, CMID), (2, 0, 1, 3))  0.9 us

profile of v3, /device:TPU:1, one launch (start us, length us, event | category | flops | bytes accessed | tf_op | source)
XLA Modules:
  0.0 38.2 jit_solution(13632296109007030695)
XLA Ops:
  0.6 0.0 copy-start.3
  0.6 1.2 %reshape.34.act = bf16[14,28,384]{2,1,0:T(8,128)(2,1)S(1)} reshape(bf16[14,14,2,384]{3,2,1,0:T(2,128)(2,1)} %bitcast.18) | data formatting | bytes 602112 | tf_op jit(solution)/shard_map/reshape | solution.py:377
  1.8 0.0 copy-start
  1.8 0.0 copy-start.1
  1.8 0.0 copy-start.2
  1.8 0.0 copy-start.4
  1.9 1.1 %reshape.35.cot = bf16[14,28,384]{2,1,0:T(8,128)(2,1)S(1)} reshape(bf16[14,14,2,384]{3,2,1,0:T(2,128)(2,1)} %bitcast.19) | data formatting | bytes 602112 | tf_op jit(solution)/shard_map/reshape | solution.py:377
  3.0 0.0 copy-done.3
  3.0 0.0 copy-done
  3.0 0.0 copy-done.1
  3.0 0.0 copy-done.2
  3.0 0.0 copy-done.4
  3.0 32.7 %shard_map.110 = (bf16[14,28,384]{2,1,0:T(8,128)(2,1)S(1)}, f32[108,128]{1,0:T(8,128)S(1)}, bf16[384,1152]{1,0:T(8,128)(2,1)S(1)}) custom-call(bf16[14,28,384]{2,1,0:T(8,128)(2,1)S(1)} %reshape.34.act, bf16[14,28,384]{2,1,0:T(8,128)(2,1)S(1)} %reshape.35.cot, bf16[384,1152]{1,0:T(8,128)(2,1)S(1)} %copy-done.3, f32[3,128]{1,0:T(4,128)S(1)} %bitcast.17, ...), custom_call_target="tpu_custom_call" | custom-call | flops 1100000000 | bytes 4000000 | tf_op jit(solution)/shard_map/pallas_call | solution.py:380
  35.7 0.9 %reshape.40 = bf16[14,14,2,384]{3,2,1,0:T(2,128)(2,1)} reshape(bf16[14,28,384]{2,1,0:T(8,128)(2,1)S(1)} %get-tuple-element.8) | data formatting | bytes 602112 | tf_op jit(solution)/shard_map/reshape | solution.py:421
  36.6 0.7 %multiply_subtract_fusion = (f32[13824]{0:T(1024)}, f32[13824]{0:T(1024)}, f32[13824]{0:T(1024)}) fusion(f32[13824]{0:T(1024)S(1)} %copy-done, f32[108,128]{1,0:T(8,128)S(1)} %get-tuple-element.9, f32[13824]{0:T(1024)S(1)} %copy-done.1, f32[13824]{0:T(1024)S(1)} %copy-done.2), kind=kLoop, calls=%fused_computation.4 | loop fusion | flops 179712 | bytes 387072 | tf_op jit(solution)/shard_map/sub | solution.py:90
  37.3 0.9 %copy.13 = bf16[384,1152]{1,0:T(8,128)(2,1)} copy(bf16[384,1152]{1,0:T(8,128)(2,1)S(1)} %get-tuple-element.23) | data formatting | bytes 1769472
Async XLA Ops:
  0.6 2.3 %copy-start.3 = (bf16[384,1152]{1,0:T(8,128)(2,1)S(1)}, bf16[384,1152]{1,0:T(8,128)(2,1)}, u32[]{:S(2)}) copy-start(bf16[384,1152]{1,0:T(8,128)(2,1)} %ker.1) | copy-start | bytes 2654212
  1.8 1.2 %copy-start = (f32[13824]{0:T(1024)S(1)}, f32[13824]{0:T(1024)}, u32[]{:S(2)}) copy-start(f32[13824]{0:T(1024)} %param.11) | copy-start | bytes 165892
  1.8 1.2 %copy-start.1 = (f32[13824]{0:T(1024)S(1)}, f32[13824]{0:T(1024)}, u32[]{:S(2)}) copy-start(f32[13824]{0:T(1024)} %param.12) | copy-start | bytes 165892
  1.8 1.2 %copy-start.2 = (f32[13824]{0:T(1024)S(1)}, f32[13824]{0:T(1024)}, u32[]{:S(2)}) copy-start(f32[13824]{0:T(1024)} %param.13) | copy-start | bytes 165892
  1.8 1.2 %copy-start.4 = (f32[384]{0:T(512)S(1)}, f32[384]{0:T(512)}, u32[]{:S(2)}) copy-start(f32[384]{0:T(512)} %param.10) | copy-start | bytes 4612

commit v4 on v3

--- a/solution.py
+++ b/solution.py
@@ -145,7 +145,7 @@
 def step_kernel(
     act, cot, ker, gain, master, mean, square,
     back, grad_out, ker_out,
-    pad32, cot32, xl, gl, gf, gb, r1, s1, r2, s3, r4, kb, kf, rows_in, rows_out,
+    pad32, cot32, pre, xl, gl, gf, gb, r1, s1, r2, s2, r3, s3, r4, kb, kf, rows_in, rows_out,
     rs_send, rs_recv, ag_send, ag_recv,
 ):
     dp = lax.axis_index("dp")
@@ -154,21 +154,20 @@
     core_dev = (dp + 1 - 2 * c, x)
     x_dev = (dp, 1 - x)
     y_dev = (dp + 2 - 4 * y, x)
-    cross_dev = (dp + 2 - 4 * y, 1 - x)
 
     def z_dev(other):
         return (other * 4 + lax.rem(dp, 4), x)
 
-    def ahead(k):
-        return lax.rem(z + k, 4)
-
-    def behind(k):
-        return lax.rem(z + 4 - k, 4)
+    z_high, z_low = lax.div(z, 2), lax.rem(z, 2)
+
+    def partner(k):
+        high = 1 - z_high if k >= 2 else z_high
+        low = 1 - z_low if k % 2 == 1 else z_low
+        return 2 * high + low
 
     barrier = pltpu.get_barrier_semaphore()
-    plane = (x_dev, y_dev, cross_dev)
-    line = tuple(z_dev(ahead(k)) for k in (1, 2, 3))
-    for device in (core_dev, *plane, *line):
+    line = tuple(z_dev(partner(k)) for k in range(4))
+    for device in (core_dev, x_dev, y_dev, *line[1:]):
         pl.semaphore_signal(barrier, inc=1, device_id=device, device_id_type=MESH)
 
     for wide_ref, narrow in ((pad32, act), (cot32, cot)):
@@ -188,7 +187,7 @@
     def window(ref, top, g):
         return ref[top : top + 14, :, g * 384 : g * 384 + 384].reshape(448, 384)
 
-    def gradient_group(g):
+    def forward_group(g):
         chans = slice(g * CG, g * CG + CG)
         image = pad32[:, :, chans].reshape(448, CG)
         for kx in range(3):
@@ -200,14 +199,18 @@
                 window(xl, ky, g), ker[chans, ky * 384 : ky * 384 + 384],
                 (((1,), (1,)), ((), ())), preferred_element_type=F32,
             )
-        rounded = (cot32[:, :, chans].reshape(448, CG) * gelu_slope(preact)).astype(BF16)
+        pre[g] = preact
+
+    def gradient_group(g):
+        chans = slice(g * CG, g * CG + CG)
+        rounded = (cot32[:, :, chans].reshape(448, CG) * gelu_slope(pre[g])).astype(BF16)
         wide = rounded.astype(F32)
         turned = wide.T.astype(BF16)
         for ky in range(3):
             part = jnp.dot(turned, window(xl, ky, g), preferred_element_type=F32)
             for kx in range(3):
-                line = g * 9 * CG + ky * 3 + kx
-                gf[pl.ds(line, CG, stride=9), :] = part[:, kx * CG : kx * CG + CG]
+                at = g * 9 * CG + ky * 3 + kx
+                gf[pl.ds(at, CG, stride=9), :] = part[:, kx * CG : kx * CG + CG]
         for kx in range(3):
             at = g * 384 + kx * CG
             gl[1:15, :, at : at + CG] = grid(shifted(wide, kx - 1))
@@ -238,59 +241,62 @@
 
     copies = {}
 
-    def pair_stage(zc):
+    def first_stage(k):
+        copies[1, k].wait_recv()
+        zc = partner(k)
+        for yc in range(2):
+            for xc in range(2):
+                one, two = (xc, yc) if k % 2 == 0 else (yc, xc)
+                s1[k, one, two] = both(gb[zc, c, yc, xc], r1[k, yc, xc]).astype(BF16)
+        mine, device = (x, x_dev) if k % 2 == 0 else (y, y_dev)
+        copies[2, k] = send(
+            s1.at[k, 1 - mine], r2.at[k], rs_send.at[1, k], rs_recv.at[1, k], device
+        )
+
+    def second_stage(k):
+        copies[2, k].wait_recv()
+        one, two, device = (x, y, y_dev) if k % 2 == 0 else (y, x, x_dev)
+        for b in range(2):
+            s2[k, b] = both(s1[k, one, b], r2[k, b]).astype(BF16)
+        copies[3, k] = send(
+            s2.at[k, 1 - two], r3.at[k], rs_send.at[2, k], rs_recv.at[2, k], device
+        )
+
+    def plane_sum(k):
+        copies[3, k].wait_recv()
+        return both(s2[k, y if k % 2 == 0 else x], r3[k])
+
+    forward_group(0)
+    forward_group(1)
+    gradient_group(0)
+    forward_group(2)
+    gradient_group(1)
+    gradient_group(2)
+    for zc in range(4):
         for yc in range(2):
             for cc in range(2):
                 for xc in range(2):
                     first = (((zc * 2 + yc) * 2 + cc) * 2 + xc) * LINES
                     gb[zc, cc, yc, xc] = gf[first : first + SLOT, :].astype(BF16)
-        copies[1, zc] = send(
-            gb.at[zc, 1 - c], r1.at[zc], rs_send.at[0, zc], rs_recv.at[0, zc], core_dev
-        )
-
-    def plane_stage(k):
-        zc = ahead(k)
-        remote(
-            gb.at[zc, 1 - c], r1.at[zc], rs_send.at[0, zc], rs_recv.at[0, zc], core_dev
-        ).wait_recv()
-        for yc in range(2):
-            for xc in range(2):
-                s1[k, yc, xc] = both(gb[zc, c, yc, xc], r1[zc, yc, xc]).astype(BF16)
-        parts = (s1.at[k, y, 1 - x], s1.at[k, 1 - y, x], s1.at[k, 1 - y, 1 - x])
-        for j in range(3):
-            copies[2 + j, k] = send(
-                parts[j], r2.at[k, j], rs_send.at[1 + j, k], rs_recv.at[1 + j, k], plane[j]
-            )
-
-    def plane_sum(k):
-        total = s1[k, y, x].astype(F32)
-        for j in range(3):
-            copies[2 + j, k].wait_recv()
-            total = total + r2[k, j].astype(F32)
-        return total
-
-    gradient_group(0)
-    pl.semaphore_wait(barrier, 7)
-    pair_stage(0)
-    gradient_group(1)
-    pair_stage(1)
-    gradient_group(2)
-    pair_stage(2)
-    pair_stage(3)
+    pl.semaphore_wait(barrier, 6)
+    order = (3, 2, 1, 0)
+    for k in order:
+        copies[1, k] = send(
+            gb.at[partner(k), 1 - c], r1.at[k], rs_send.at[0, k], rs_recv.at[0, k], core_dev
+        )
     input_back_group(0)
-    order = (2, 1, 3, 0)
     for k in order:
-        plane_stage(k)
+        first_stage(k)
     input_back_group(1)
-    for k in order[0:3]:
+    for k in order:
+        second_stage(k)
+    input_back_group(2)
+    for k in (3, 2, 1):
         s3[k] = plane_sum(k).astype(BF16)
-        copies[5, k] = send(
-            s3.at[k], r4.at[k], rs_send.at[4, k], rs_recv.at[4, k], line[k - 1]
-        )
+        copies[4, k] = send(s3.at[k], r4.at[k], rs_send.at[3, k], rs_recv.at[3, k], line[k])
     grad = plane_sum(0)
-    input_back_group(2)
-    for k in (1, 3, 2):
-        copies[5, k].wait_recv()
+    for k in (1, 2, 3):
+        copies[4, k].wait_recv()
         grad = grad + r4[k].astype(F32)
     grad = grad[0:LINES, :]
     grad_out[...] = grad
@@ -317,30 +323,31 @@
         rows_out[pl.ds(t, SHARD_ROWS, stride=9), :] = (taps[t] - chan_mean) * chan_scale
     kb[z, c, y, x] = rows_out[...].astype(BF16)
 
-    def spread(k, slot, step, device):
+    def spread(k, step, slot, device):
         copies[step, k] = send(
-            slot, slot, ag_send.at[step - 6, k], ag_recv.at[step - 6, k], device
+            slot, slot, ag_send.at[step - 5, k], ag_recv.at[step - 5, k], device
         )
 
     def spread_own(k):
-        slot = kb.at[behind(k), c, y, x]
         if k != 0:
-            copies[6, k].wait_recv()
-        for j in range(3):
-            spread(k, slot, 7 + j, plane[j])
-        spread(k, slot, 10, core_dev)
-
-    def relay(k):
-        held = kb.at[behind(k), c]
-        slots = (held.at[y, 1 - x], held.at[1 - y, x], held.at[1 - y, 1 - x])
-        for j in range(3):
-            copies[7 + j, k].wait_recv()
-            spread(k, slots[j], 11 + j, core_dev)
+            copies[5, k].wait_recv()
+        spread(k, 6, kb.at[partner(k), c, y, x], x_dev if k % 2 == 0 else y_dev)
+
+    def spread_two(k):
+        copies[6, k].wait_recv()
+        held = kb.at[partner(k), c]
+        if k % 2 == 0:
+            spread(k, 7, held.at[y], y_dev)
+        else:
+            spread(k, 7, held.at[:, x], x_dev)
+
+    def spread_four(k):
+        copies[7, k].wait_recv()
+        spread(k, 8, kb.at[partner(k), c], core_dev)
 
     def finish(k):
-        for step in range(10, 14):
-            copies[step, k].wait_recv()
-        zc = behind(k)
+        copies[8, k].wait_recv()
+        zc = partner(k)
         for yc in range(2):
             for cc in range(2):
                 for xc in range(2):
@@ -350,20 +357,24 @@
         for t in range(9):
             ker_out[rows, t * CG : t * CG + CG] = kf[pl.ds(t, 96, stride=9), :].astype(BF16)
 
-    for k in (2, 1, 3):
-        spread(k, kb.at[z, c, y, x], 6, line[k - 1])
+    for k in (3, 2, 1):
+        spread(k, 5, kb.at[z, c, y, x], line[k])
     spread_own(0)
     spread_own(1)
-    relay(0)
+    spread_two(0)
+    spread_own(2)
+    spread_two(1)
+    spread_four(0)
     spread_own(3)
-    relay(1)
-    spread_own(2)
-    relay(3)
+    spread_two(2)
+    spread_four(1)
     finish(0)
-    relay(2)
+    spread_two(3)
+    spread_four(2)
     finish(1)
+    spread_four(3)
+    finish(2)
     finish(3)
-    finish(2)
     for copy in copies.values():
         copy.wait_send()
 
@@ -389,23 +400,26 @@
         scratch_shapes=[
             pltpu.VMEM((14, 32, CMID), F32),
             pltpu.VMEM((14, 32, CMID), F32),
+            pltpu.VMEM((GROUPS, 448, CG), F32),
             pltpu.VMEM((16, 32, 9 * CG), BF16),
             pltpu.VMEM((16, 32, 9 * CG), BF16),
             pltpu.VMEM((3472, CG), F32),
             pltpu.VMEM((4, 2, 2, 2, SLOT, CG), BF16),
             pltpu.VMEM((4, 2, 2, SLOT, CG), BF16),
             pltpu.VMEM((4, 2, 2, SLOT, CG), BF16),
-            pltpu.VMEM((4, 3, SLOT, CG), BF16),
+            pltpu.VMEM((4, 2, SLOT, CG), BF16),
+            pltpu.VMEM((4, 2, SLOT, CG), BF16),
+            pltpu.VMEM((4, SLOT, CG), BF16),
             pltpu.VMEM((4, SLOT, CG), BF16),
             pltpu.VMEM((4, SLOT, CG), BF16),
             pltpu.VMEM((4, 2, 2, 2, SLOT, CG), BF16),
             pltpu.VMEM((96 * 9, CG), F32),
             pltpu.VMEM((SLOT, CG), F32),
             pltpu.VMEM((SLOT, CG), F32),
-            pltpu.SemaphoreType.DMA((5, 4)),
-            pltpu.SemaphoreType.DMA((5, 4)),
-            pltpu.SemaphoreType.DMA((8, 4)),
-            pltpu.SemaphoreType.DMA((8, 4)),
+            pltpu.SemaphoreType.DMA((4, 4)),
+            pltpu.SemaphoreType.DMA((4, 4)),
+            pltpu.SemaphoreType.DMA((4, 4)),
+            pltpu.SemaphoreType.DMA((4, 4)),
         ],
         compiler_params=pltpu.CompilerParams(
             collective_id=0, has_side_effects=True, vmem_limit_bytes=40 * 1024 * 1024

time: 38.3 us -> 36.9 us (0.963)
  Pallas kernels: 32.7 us -> 31.2 us
    pallas_call x1, Pallas kernels: 32.7 us -> 31.2 us  [fused_on_device(): pl.pallas_call(step_kernel, out_shape=(jax.ShapeDtypeStruct((side, side *...]
where the time goes in v4:
time: 36.9 us; the launch traced here: 36.7 us
  Pallas kernels  31.2 us (85%)
  local copies, waits for them, and re-layouts  4.1 us (11%)
  between operations  0.73 us (2%)
  other arithmetic  0.68 us (2%)
    pallas_call x1, Pallas kernels, fused_on_device(): pl.pallas_call(step_kernel, out_shape=(jax.ShapeDtypeStruct((side, side *...  31.2 us
    reshape x2, local copies, waits for them, and re-layouts, by_place(): return jnp.transpose(images, (1, 2, 0, 3)).reshape(side, side * 2, CMID)  2.26 us
    unnamed x11, local copies, waits for them, and re-layouts  0.94 us
    reshape x1, local copies, waits for them, and re-layouts, fused_on_device(): input_grad = jnp.transpose(back.reshape(side, side, 2, CMID), (2, 0, 1, 3))  0.9 us

profile of v4, /device:TPU:1, one launch (start us, length us, event | category | flops | bytes accessed | tf_op | source)
XLA Modules:
  0.0 36.7 jit_solution(1786949517019123864)
XLA Ops:
  0.6 0.0 copy-start.3
  0.6 1.2 %reshape.34.act = bf16[14,28,384]{2,1,0:T(8,128)(2,1)S(1)} reshape(bf16[14,14,2,384]{3,2,1,0:T(2,128)(2,1)} %bitcast.18) | data formatting | bytes 602112 | tf_op jit(solution)/shard_map/reshape | solution.py:388
  1.8 0.0 copy-start
  1.8 0.0 copy-start.1
  1.8 0.0 copy-start.2
  1.8 0.0 copy-start.4
  1.9 1.1 %reshape.35.cot = bf16[14,28,384]{2,1,0:T(8,128)(2,1)S(1)} reshape(bf16[14,14,2,384]{3,2,1,0:T(2,128)(2,1)} %bitcast.19) | data formatting | bytes 602112 | tf_op jit(solution)/shard_map/reshape | solution.py:388
  3.0 0.0 copy-done.3
  3.0 0.0 copy-done
  3.0 0.0 copy-done.1
  3.0 0.0 copy-done.2
  3.0 0.0 copy-done.4
  3.0 31.2 %shard_map.110 = (bf16[14,28,384]{2,1,0:T(8,128)(2,1)S(1)}, f32[108,128]{1,0:T(8,128)S(1)}, bf16[384,1152]{1,0:T(8,128)(2,1)S(1)}) custom-call(bf16[14,28,384]{2,1,0:T(8,128)(2,1)S(1)} %reshape.34.act, bf16[14,28,384]{2,1,0:T(8,128)(2,1)S(1)} %reshape.35.cot, bf16[384,1152]{1,0:T(8,128)(2,1)S(1)} %copy-done.3, f32[3,128]{1,0:T(4,128)S(1)} %bitcast.17, ...), custom_call_target="tpu_custom_call" | custom-call | flops 1100000000 | bytes 4000000 | tf_op jit(solution)/shard_map/pallas_call | solution.py:391
  34.2 0.9 %reshape.40 = bf16[14,14,2,384]{3,2,1,0:T(2,128)(2,1)} reshape(bf16[14,28,384]{2,1,0:T(8,128)(2,1)S(1)} %get-tuple-element.8) | data formatting | bytes 602112 | tf_op jit(solution)/shard_map/reshape | solution.py:435
  35.1 0.7 %multiply_subtract_fusion = (f32[13824]{0:T(1024)}, f32[13824]{0:T(1024)}, f32[13824]{0:T(1024)}) fusion(f32[13824]{0:T(1024)S(1)} %copy-done, f32[108,128]{1,0:T(8,128)S(1)} %get-tuple-element.9, f32[13824]{0:T(1024)S(1)} %copy-done.1, f32[13824]{0:T(1024)S(1)} %copy-done.2), kind=kLoop, calls=%fused_computation.4 | loop fusion | flops 179712 | bytes 387072 | tf_op jit(solution)/shard_map/sub | solution.py:90
  35.8 0.9 %copy.13 = bf16[384,1152]{1,0:T(8,128)(2,1)} copy(bf16[384,1152]{1,0:T(8,128)(2,1)S(1)} %get-tuple-element.23) | data formatting | bytes 1769472
Async XLA Ops:
  0.6 2.3 %copy-start.3 = (bf16[384,1152]{1,0:T(8,128)(2,1)S(1)}, bf16[384,1152]{1,0:T(8,128)(2,1)}, u32[]{:S(2)}) copy-start(bf16[384,1152]{1,0:T(8,128)(2,1)} %ker.1) | copy-start | bytes 2654212
  1.8 1.2 %copy-start = (f32[13824]{0:T(1024)S(1)}, f32[13824]{0:T(1024)}, u32[]{:S(2)}) copy-start(f32[13824]{0:T(1024)} %param.11) | copy-start | bytes 165892
  1.8 1.2 %copy-start.1 = (f32[13824]{0:T(1024)S(1)}, f32[13824]{0:T(1024)}, u32[]{:S(2)}) copy-start(f32[13824]{0:T(1024)} %param.12) | copy-start | bytes 165892
  1.8 1.2 %copy-start.2 = (f32[13824]{0:T(1024)S(1)}, f32[13824]{0:T(1024)}, u32[]{:S(2)}) copy-start(f32[13824]{0:T(1024)} %param.13) | copy-start | bytes 165892
  1.8 1.2 %copy-start.4 = (f32[384]{0:T(512)S(1)}, f32[384]{0:T(512)}, u32[]{:S(2)}) copy-start(f32[384]{0:T(512)} %param.10) | copy-start | bytes 4612

commit v5 on v1

--- a/solution.py
+++ b/solution.py
@@ -81,6 +81,15 @@
     return (chan_mean, channel_gain / jnp.sqrt(FAN * chan_var + 0.0001))
 
 
+def adam(grad, master, mean, square):
+    mean_next = 0.9 * mean + 0.1 * grad
+    square_next = 0.999 * square + 0.001 * grad * grad
+    fix_mean = 1.0 - 0.9**ADAM_STEP
+    fix_square = 1.0 - 0.999**ADAM_STEP
+    update = mean_next / fix_mean / (jnp.sqrt(square_next / fix_square) + 1e-08)
+    return (master - 0.02 * update, mean_next, square_next)
+
+
 def on_device(
     activations, cotangent, kernel, channel_gain, master_flat, moment_mean, moment_square
 ):
@@ -90,12 +99,9 @@
     grad_full = kernel_back(activations, pre_grad)
     grad_shard = lax.psum_scatter(grad_full, ("dp", "sub"), scatter_dimension=0, tiled=True)
     input_grad = input_back(pre_grad, kernel_taps).astype(jnp.bfloat16)
-    mean_next = 0.9 * moment_mean + 0.1 * grad_shard
-    square_next = 0.999 * moment_square + 0.001 * grad_shard * grad_shard
-    fix_mean = 1.0 - 0.9**ADAM_STEP
-    fix_square = 1.0 - 0.999**ADAM_STEP
-    update = mean_next / fix_mean / (jnp.sqrt(square_next / fix_square) + 1e-08)
-    master_next = master_flat - 0.02 * update
+    master_next, mean_next, square_next = adam(
+        grad_shard, master_flat, moment_mean, moment_square
+    )
     shard_len = master_next.shape[0]
     shard_start = lax.axis_index(("dp", "sub")) * shard_len
     first_chan = shard_start // FAN
@@ -138,7 +144,7 @@
 
 def step_kernel(
     act, cot, ker, gain, master, mean, square,
-    back, master_out, mean_out, square_out, ker_out,
+    back, grad_out, ker_out,
     pad32, cot32, xl, gl, gf, gb, r1, s1, r2, s2, r3, s3, r4, kb, kf, rows_in, rows_out,
     rs_send, rs_recv, ag_send, ag_recv,
 ):
@@ -274,27 +280,22 @@
         copies[4, k].wait_recv()
         grad = grad + r4[k].astype(F32)
     grad = grad[0:LINES, :]
-
-    mean_next = 0.9 * mean[...] + 0.1 * grad
-    square_next = 0.999 * square[...] + 0.001 * grad * grad
-    fix_mean = 1.0 - 0.9**ADAM_STEP
-    fix_square = 1.0 - 0.999**ADAM_STEP
-    update = mean_next / fix_mean / (jnp.sqrt(square_next / fix_square) + 1e-08)
-    master_next = master[...] - 0.02 * update
-    mean_out[...] = mean_next
-    square_out[...] = square_next
-    master_out[...] = master_next
+    grad_out[...] = grad
+
+    master_next, _, _ = adam(grad, master[...], mean[...], square[...])
     rows_in[0:LINES, :] = master_next
     taps = [rows_in[pl.ds(t, SHARD_ROWS, stride=9), :] for t in range(9)]
     plain, squares = taps[0], taps[0] * taps[0]
     for tap in taps[1:]:
         plain, squares = plain + tap, squares + tap * tap
-    shape = (SHARD_ROWS, CMID)
+    shape = (SHARD_ROWS, CG)
     first_chan = (dp * 2 + x) * SHARD_ROWS
-    own = lax.broadcasted_iota(jnp.int32, shape, 1) == (
-        lax.broadcasted_iota(jnp.int32, shape, 0) + first_chan
-    )
-    own_gain = jnp.sum(jnp.where(own, gain[...], 0.0), axis=1, keepdims=True)
+    chan = lax.broadcasted_iota(jnp.int32, shape, 0) + first_chan
+    lane = lax.broadcasted_iota(jnp.int32, shape, 1)
+    picked = jnp.zeros(shape, F32)
+    for g in range(GROUPS):
+        picked += jnp.where(lane + g * CG == chan, gain[g : g + 1, :], 0.0)
+    own_gain = jnp.sum(picked, axis=1, keepdims=True)
     chan_mean, chan_scale = channel_scale(
         jnp.sum(plain, axis=1, keepdims=True), jnp.sum(squares, axis=1, keepdims=True), own_gain
     )
@@ -346,18 +347,15 @@
     activations, cotangent, kernel, channel_gain, master_flat, moment_mean, moment_square
 ):
     vmem = pl.BlockSpec(memory_space=pltpu.VMEM)
-    lines = jax.ShapeDtypeStruct((LINES, CG), F32)
-    back, master_next, mean_next, square_next, kernel_next = pl.pallas_call(
+    back, grad, kernel_next = pl.pallas_call(
         step_kernel,
         out_shape=(
             jax.ShapeDtypeStruct(activations.shape, BF16),
-            lines,
-            lines,
-            lines,
+            jax.ShapeDtypeStruct((LINES, CG), F32),
             jax.ShapeDtypeStruct((CMID, FAN), BF16),
         ),
         in_specs=[vmem] * 7,
-        out_specs=(vmem,) * 5,
+        out_specs=(vmem,) * 3,
         scratch_shapes=[
             pltpu.VMEM((2, 14, 16, CMID), F32),
             pltpu.VMEM((2, 14, 16, CMID), F32),
@@ -388,13 +386,14 @@
             flops=1_100_000_000, bytes_accessed=4_000_000, transcendentals=400_000
         ),
     )(
-        activations, cotangent, kernel, channel_gain.reshape(1, CMID),
+        activations, cotangent, kernel, channel_gain.reshape(GROUPS, CG),
         master_flat.reshape(LINES, CG), moment_mean.reshape(LINES, CG),
         moment_square.reshape(LINES, CG),
     )
-    return (
-        back, master_next.reshape(-1), mean_next.reshape(-1), square_next.reshape(-1), kernel_next
-    )
+    master_next, mean_next, square_next = adam(
+        grad.reshape(-1), master_flat, moment_mean, moment_square
+    )
+    return (back, master_next, mean_next, square_next, kernel_next)
 
 
 def solution(mesh):

time: 38 us -> 36.1 us (0.950)
  local copies, waits for them, and re-layouts: 6.59 us -> 4.01 us
  other arithmetic: 0 us -> 0.68 us
    unnamed x15 -> x14, local copies, waits for them, and re-layouts: 5.83 us -> 4.01 us
    reshape x1 -> x0, local copies, waits for them, and re-layouts: 0.76 us -> none  [fused_on_device(): channel_gain.reshape(1, CMID)]
    sub x0 -> x1, other arithmetic: none -> 0.68 us  [adam(): return (master - 0.02 * update, mean_next, square_next)]
where the time goes in v5:
time: 36.1 us; the launch traced here: 35.9 us
  Pallas kernels  30.5 us (84%)
  local copies, waits for them, and re-layouts  4.01 us (11%)
  between operations  0.73 us (2%)
  other arithmetic  0.68 us (2%)
    pallas_call x1, Pallas kernels, fused_on_device(): pl.pallas_call(step_kernel, out_shape=(jax.ShapeDtypeStruct(activations.s...  30.5 us
    unnamed x14, local copies, waits for them, and re-layouts  4.01 us

profile of v5, /device:TPU:1, one launch (start us, length us, event | category | flops | bytes accessed | tf_op | source)
XLA Modules:
  0.0 35.9 jit_solution(6861978668950142725)
XLA Ops:
  0.6 0.0 copy-start.3
  0.6 1.1 %copy.12.act = bf16[2,14,14,384]{3,2,1,0:T(8,128)(2,1)S(1)} copy(bf16[2,14,14,384]{3,0,2,1:T(2,128)(2,1)} %param.7) | data formatting | bytes 602112 | tf_op args[0]
  1.7 0.0 copy-start
  1.7 0.0 copy-start.1
  1.8 0.0 copy-start.2
  1.8 0.0 copy-start.4
  1.8 1.0 %copy.13.cot = bf16[2,14,14,384]{3,2,1,0:T(8,128)(2,1)S(1)} copy(bf16[2,14,14,384]{3,0,2,1:T(2,128)(2,1)} %param.8) | data formatting | bytes 602112 | tf_op args[1]
  2.8 0.0 copy-done.3
  2.8 0.0 copy-done
  2.8 0.0 copy-done.1
  2.8 0.0 copy-done.2
  2.9 0.0 copy-done.4
  2.9 30.5 %shard_map.110 = (bf16[2,14,14,384]{3,2,1,0:T(8,128)(2,1)S(1)}, f32[108,128]{1,0:T(8,128)S(1)}, bf16[384,1152]{1,0:T(8,128)(2,1)S(1)}) custom-call(bf16[2,14,14,384]{3,2,1,0:T(8,128)(2,1)S(1)} %copy.12.act, bf16[2,14,14,384]{3,2,1,0:T(8,128)(2,1)S(1)} %copy.13.cot, bf16[384,1152]{1,0:T(8,128)(2,1)S(1)} %copy-done.3, f32[3,128]{1,0:T(4,128)S(1)} %bitcast.14, ...), custom_call_target="tpu_custom_call" | custom-call | flops 1100000000 | bytes 4000000 | tf_op jit(solution)/shard_map/pallas_call | solution.py:350
  33.4 0.9 %copy.14 = bf16[2,14,14,384]{3,0,2,1:T(2,128)(2,1)} copy(bf16[2,14,14,384]{3,2,1,0:T(8,128)(2,1)S(1)} %get-tuple-element.11) | data formatting | bytes 602112
  34.3 0.7 %multiply_subtract_fusion = (f32[13824]{0:T(1024)}, f32[13824]{0:T(1024)}, f32[13824]{0:T(1024)}) fusion(f32[13824]{0:T(1024)S(1)} %copy-done, f32[108,128]{1,0:T(8,128)S(1)} %get-tuple-element.9, f32[13824]{0:T(1024)S(1)} %copy-done.1, f32[13824]{0:T(1024)S(1)} %copy-done.2), kind=kLoop, calls=%fused_computation.4 | loop fusion | flops 179712 | bytes 387072 | tf_op jit(solution)/shard_map/sub | solution.py:90
  35.0 0.9 %copy.16 = bf16[384,1152]{1,0:T(8,128)(2,1)} copy(bf16[384,1152]{1,0:T(8,128)(2,1)S(1)} %get-tuple-element.28) | data formatting | bytes 1769472
Async XLA Ops:
  0.6 2.2 %copy-start.3 = (bf16[384,1152]{1,0:T(8,128)(2,1)S(1)}, bf16[384,1152]{1,0:T(8,128)(2,1)}, u32[]{:S(2)}) copy-start(bf16[384,1152]{1,0:T(8,128)(2,1)} %ker.1) | copy-start | bytes 2654212
  1.7 1.1 %copy-start = (f32[13824]{0:T(1024)S(1)}, f32[13824]{0:T(1024)}, u32[]{:S(2)}) copy-start(f32[13824]{0:T(1024)} %param.11) | copy-start | bytes 165892
  1.7 1.1 %copy-start.1 = (f32[13824]{0:T(1024)S(1)}, f32[13824]{0:T(1024)}, u32[]{:S(2)}) copy-start(f32[13824]{0:T(1024)} %param.12) | copy-start | bytes 165892
  1.8 1.1 %copy-start.2 = (f32[13824]{0:T(1024)S(1)}, f32[13824]{0:T(1024)}, u32[]{:S(2)}) copy-start(f32[13824]{0:T(1024)} %param.13) | copy-start | bytes 165892
  1.8 1.1 %copy-start.4 = (f32[384]{0:T(512)S(1)}, f32[384]{0:T(512)}, u32[]{:S(2)}) copy-start(f32[384]{0:T(512)} %param.10) | copy-start | bytes 4612

commit v6 on v2

--- a/solution.py
+++ b/solution.py
@@ -81,6 +81,15 @@
     return (chan_mean, channel_gain / jnp.sqrt(FAN * chan_var + 0.0001))
 
 
+def adam(grad, master, mean, square):
+    mean_next = 0.9 * mean + 0.1 * grad
+    square_next = 0.999 * square + 0.001 * grad * grad
+    fix_mean = 1.0 - 0.9**ADAM_STEP
+    fix_square = 1.0 - 0.999**ADAM_STEP
+    update = mean_next / fix_mean / (jnp.sqrt(square_next / fix_square) + 1e-08)
+    return (master - 0.02 * update, mean_next, square_next)
+
+
 def on_device(
     activations, cotangent, kernel, channel_gain, master_flat, moment_mean, moment_square
 ):
@@ -90,12 +99,9 @@
     grad_full = kernel_back(activations, pre_grad)
     grad_shard = lax.psum_scatter(grad_full, ("dp", "sub"), scatter_dimension=0, tiled=True)
     input_grad = input_back(pre_grad, kernel_taps).astype(jnp.bfloat16)
-    mean_next = 0.9 * moment_mean + 0.1 * grad_shard
-    square_next = 0.999 * moment_square + 0.001 * grad_shard * grad_shard
-    fix_mean = 1.0 - 0.9**ADAM_STEP
-    fix_square = 1.0 - 0.999**ADAM_STEP
-    update = mean_next / fix_mean / (jnp.sqrt(square_next / fix_square) + 1e-08)
-    master_next = master_flat - 0.02 * update
+    master_next, mean_next, square_next = adam(
+        grad_shard, master_flat, moment_mean, moment_square
+    )
     shard_len = master_next.shape[0]
     shard_start = lax.axis_index(("dp", "sub")) * shard_len
     first_chan = shard_start // FAN
@@ -138,7 +144,7 @@
 
 def step_kernel(
     act, cot, ker, gain, master, mean, square,
-    back, master_out, mean_out, square_out, ker_out,
+    back, grad_out, ker_out,
     pad32, cot32, xl, gl, gf, gb, r1, s1, r2, s2, r3, s3, held, r4, kb, kf, rows_in, rows_out,
     rs_send, rs_recv, ag_send, ag_recv,
 ):
@@ -277,25 +283,26 @@
             line_copy(z, zc).start()
 
     gradient_group(0)
+    gradient_group(1)
     pl.semaphore_wait(barrier, 6)
     pair_stage(0)
-    gradient_group(1)
     pair_stage(1)
-    first_stage(0)
     gradient_group(2)
     pair_stage(2)
     pair_stage(3)
+    first_stage(0)
     first_stage(1)
-    second_stage(0)
+    input_back_group(0)
     first_stage(2)
     first_stage(3)
-    input_back_group(0)
+    second_stage(0)
     second_stage(1)
+    input_back_group(1)
     line_stage(0)
+    line_stage(1)
     second_stage(2)
     second_stage(3)
-    input_back_group(1)
-    line_stage(1)
+    input_back_group(2)
     line_stage(2)
     line_stage(3)
     grad = held[z]
@@ -303,16 +310,9 @@
         line_copy(ahead(k), ahead(k)).wait_recv()
         grad = grad + r4[ahead(k)].astype(F32)
     grad = grad[0:LINES, :]
-
-    mean_next = 0.9 * mean[...] + 0.1 * grad
-    square_next = 0.999 * square[...] + 0.001 * grad * grad
-    fix_mean = 1.0 - 0.9**ADAM_STEP
-    fix_square = 1.0 - 0.999**ADAM_STEP
-    update = mean_next / fix_mean / (jnp.sqrt(square_next / fix_square) + 1e-08)
-    master_next = master[...] - 0.02 * update
-    mean_out[...] = mean_next
-    square_out[...] = square_next
-    master_out[...] = master_next
+    grad_out[...] = grad
+
+    master_next, _, _ = adam(grad, master[...], mean[...], square[...])
     rows_in[0:LINES, :] = master_next
     taps = [rows_in[pl.ds(t, SHARD_ROWS, stride=9), :] for t in range(9)]
     plain, squares = taps[0], taps[0] * taps[0]
@@ -339,7 +339,6 @@
         copies[5, k] = send(
             own_slot, own_slot, ag_send.at[0, k], ag_recv.at[0, k], z_dev(ahead(k))
         )
-    input_back_group(2)
     order = (0, 1, 3, 2)
     for k in order:
         if k != 0:
@@ -376,45 +375,19 @@
         line_copy(z, ahead(k)).wait_send()
 
 
-def copy_kernel(*refs):
-    count = (len(refs) - 1) // 2
-    sems = refs[-1]
-    copies = [
-        pltpu.make_async_copy(refs[i], refs[count + i], sems.at[i]) for i in range(count)
-    ]
-    for copy in copies:
-        copy.start()
-    for copy in copies:
-        copy.wait()
-
-
-def put_out(*results):
-    place = pl.BlockSpec(memory_space=pl.ANY)
-    return pl.pallas_call(
-        copy_kernel,
-        out_shape=tuple(jax.ShapeDtypeStruct(r.shape, r.dtype) for r in results),
-        in_specs=[place] * len(results),
-        out_specs=(place,) * len(results),
-        scratch_shapes=[pltpu.SemaphoreType.DMA((len(results),))],
-    )(*results)
-
-
 def fused_on_device(
     activations, cotangent, kernel, channel_gain, master_flat, moment_mean, moment_square
 ):
     vmem = pl.BlockSpec(memory_space=pltpu.VMEM)
-    lines = jax.ShapeDtypeStruct((LINES, CG), F32)
-    back, master_next, mean_next, square_next, kernel_next = pl.pallas_call(
+    back, grad, kernel_next = pl.pallas_call(
         step_kernel,
         out_shape=(
             jax.ShapeDtypeStruct(activations.shape, BF16),
-            lines,
-            lines,
-            lines,
+            jax.ShapeDtypeStruct((LINES, CG), F32),
             jax.ShapeDtypeStruct((CMID, FAN), BF16),
         ),
         in_specs=[vmem] * 7,
-        out_specs=(vmem,) * 5,
+        out_specs=(vmem,) * 3,
         scratch_shapes=[
             pltpu.VMEM((2, 14, 16, CMID), F32),
             pltpu.VMEM((2, 14, 16, CMID), F32),
@@ -450,12 +423,10 @@
         master_flat.reshape(LINES, CG), moment_mean.reshape(LINES, CG),
         moment_square.reshape(LINES, CG),
     )
-    master_next, mean_next, square_next, kernel_next = put_out(
-        master_next, mean_next, square_next, kernel_next
-    )
-    return (
-        back, master_next.reshape(-1), mean_next.reshape(-1), square_next.reshape(-1), kernel_next
-    )
+    master_next, mean_next, square_next = adam(
+        grad.reshape(-1), master_flat, moment_mean, moment_square
+    )
+    return (back, master_next, mean_next, square_next, kernel_next)
 
 
 def solution(mesh):

time: 73.3 us -> 38.5 us (0.53)
  Pallas kernels: 66.6 us -> 33 us
  local copies, waits for them, and re-layouts: 5.89 us -> 4.01 us
    pallas_call x1 -> x0, Pallas kernels: 33 us -> none  [put_out(): pl.pallas_call(copy_kernel, out_shape=tuple((jax.ShapeDtypeStruct(r.shape...]
    unnamed x21 -> x14, local copies, waits for them, and re-layouts: 5.89 us -> 4.01 us
where the time goes in v6:
time: 38.5 us; the launch traced here: 38.4 us
  Pallas kernels  33 us (86%)
  local copies, waits for them, and re-layouts  4.01 us (10%)
  between operations  0.73 us (2%)
  other arithmetic  0.68 us (2%)
    pallas_call x1, Pallas kernels, fused_on_device(): pl.pallas_call(step_kernel, out_shape=(jax.ShapeDtypeStruct(activations.s...  33 us
    unnamed x14, local copies, waits for them, and re-layouts  4.01 us

profile of v6, /device:TPU:1, one launch (start us, length us, event | category | flops | bytes accessed | tf_op | source)
XLA Modules:
  0.0 38.4 jit_solution(3610532470308284093)
XLA Ops:
  0.6 0.0 copy-start.3
  0.6 1.1 %copy.12.act = bf16[2,14,14,384]{3,2,1,0:T(8,128)(2,1)S(1)} copy(bf16[2,14,14,384]{3,0,2,1:T(2,128)(2,1)} %param.7) | data formatting | bytes 602112 | tf_op args[0]
  1.7 0.0 copy-start
  1.7 0.0 copy-start.1
  1.8 0.0 copy-start.2
  1.8 0.0 copy-start.4
  1.8 1.0 %copy.13.cot = bf16[2,14,14,384]{3,2,1,0:T(8,128)(2,1)S(1)} copy(bf16[2,14,14,384]{3,0,2,1:T(2,128)(2,1)} %param.8) | data formatting | bytes 602112 | tf_op args[1]
  2.8 0.0 copy-done.3
  2.8 0.0 copy-done
  2.8 0.0 copy-done.1
  2.8 0.0 copy-done.2
  2.9 0.0 copy-done.4
  2.9 33.0 %shard_map.110 = (bf16[2,14,14,384]{3,2,1,0:T(8,128)(2,1)S(1)}, f32[108,128]{1,0:T(8,128)S(1)}, bf16[384,1152]{1,0:T(8,128)(2,1)S(1)}) custom-call(bf16[2,14,14,384]{3,2,1,0:T(8,128)(2,1)S(1)} %copy.12.act, bf16[2,14,14,384]{3,2,1,0:T(8,128)(2,1)S(1)} %copy.13.cot, bf16[384,1152]{1,0:T(8,128)(2,1)S(1)} %copy-done.3, f32[3,128]{1,0:T(4,128)S(1)} %bitcast.14, ...), custom_call_target="tpu_custom_call" | custom-call | flops 1100000000 | bytes 4000000 | tf_op jit(solution)/shard_map/pallas_call | solution.py:382
  35.9 0.9 %copy.14 = bf16[2,14,14,384]{3,0,2,1:T(2,128)(2,1)} copy(bf16[2,14,14,384]{3,2,1,0:T(8,128)(2,1)S(1)} %get-tuple-element.11) | data formatting | bytes 602112
  36.8 0.7 %multiply_subtract_fusion = (f32[13824]{0:T(1024)}, f32[13824]{0:T(1024)}, f32[13824]{0:T(1024)}) fusion(f32[13824]{0:T(1024)S(1)} %copy-done, f32[108,128]{1,0:T(8,128)S(1)} %get-tuple-element.9, f32[13824]{0:T(1024)S(1)} %copy-done.1, f32[13824]{0:T(1024)S(1)} %copy-done.2), kind=kLoop, calls=%fused_computation.4 | loop fusion | flops 179712 | bytes 387072 | tf_op jit(solution)/shard_map/sub | solution.py:90
  37.5 0.9 %copy.16 = bf16[384,1152]{1,0:T(8,128)(2,1)} copy(bf16[384,1152]{1,0:T(8,128)(2,1)S(1)} %get-tuple-element.28) | data formatting | bytes 1769472
Async XLA Ops:
  0.6 2.2 %copy-start.3 = (bf16[384,1152]{1,0:T(8,128)(2,1)S(1)}, bf16[384,1152]{1,0:T(8,128)(2,1)}, u32[]{:S(2)}) copy-start(bf16[384,1152]{1,0:T(8,128)(2,1)} %ker.1) | copy-start | bytes 2654212
  1.7 1.1 %copy-start = (f32[13824]{0:T(1024)S(1)}, f32[13824]{0:T(1024)}, u32[]{:S(2)}) copy-start(f32[13824]{0:T(1024)} %param.11) | copy-start | bytes 165892
  1.7 1.1 %copy-start.1 = (f32[13824]{0:T(1024)S(1)}, f32[13824]{0:T(1024)}, u32[]{:S(2)}) copy-start(f32[13824]{0:T(1024)} %param.12) | copy-start | bytes 165892
  1.8 1.1 %copy-start.2 = (f32[13824]{0:T(1024)S(1)}, f32[13824]{0:T(1024)}, u32[]{:S(2)}) copy-start(f32[13824]{0:T(1024)} %param.13) | copy-start | bytes 165892
  1.8 1.1 %copy-start.4 = (f32[384]{0:T(512)S(1)}, f32[384]{0:T(512)}, u32[]{:S(2)}) copy-start(f32[384]{0:T(512)} %param.10) | copy-start | bytes 4612

commit v7 on v5

--- a/solution.py
+++ b/solution.py
@@ -192,23 +192,19 @@
         for kx in range(3):
             at = g * 384 + kx * CG
             xl[:, 1:15, :, at : at + CG] = grid(shifted(image, 1 - kx))
-        preact = jnp.zeros((448, CG), F32)
-        for ky in range(3):
-            preact += lax.dot_general(
-                window(xl, ky, g), ker[chans, ky * 384 : ky * 384 + 384],
-                (((1,), (1,)), ((), ())), preferred_element_type=F32,
-            )
+        windows = jnp.concatenate([window(xl, ky, g) for ky in range(3)], axis=1)
+        preact = lax.dot_general(
+            windows, ker[chans, :], (((1,), (1,)), ((), ())), preferred_element_type=F32
+        )
         rounded = (cot32[:, :, :, chans].reshape(448, CG) * gelu_slope(preact)).astype(BF16)
         wide = rounded.astype(F32)
         for kx in range(3):
             at = g * 384 + kx * CG
             gl[:, 1:15, :, at : at + CG] = grid(shifted(wide, kx - 1))
         turned = wide.T.astype(BF16)
-        for ky in range(3):
-            part = jnp.dot(turned, window(xl, ky, g), preferred_element_type=F32)
-            for kx in range(3):
-                line = g * 9 * CG + ky * 3 + kx
-                gf[pl.ds(line, CG, stride=9), :] = part[:, kx * CG : kx * CG + CG]
+        part = jnp.dot(turned, windows, preferred_element_type=F32)
+        for tap in range(9):
+            gf[pl.ds(g * 9 * CG + tap, CG, stride=9), :] = part[:, tap * CG : tap * CG + CG]
 
     for zc in range(4):
         for yc in range(2):
@@ -219,12 +215,9 @@
 
     def input_back_group(g):
         chans = slice(g * CG, g * CG + CG)
-        total = jnp.zeros((448, CG), F32)
-        for ky in range(3):
-            taps = [ker[chans, (ky * 3 + kx) * CG : (ky * 3 + kx) * CG + CG] for kx in range(3)]
-            total += jnp.dot(
-                window(gl, 2 - ky, g), jnp.concatenate(taps, axis=0), preferred_element_type=F32
-            )
+        windows = jnp.concatenate([window(gl, 2 - ky, g) for ky in range(3)], axis=1)
+        taps = [ker[chans, tap * CG : tap * CG + CG] for tap in range(9)]
+        total = jnp.dot(windows, jnp.concatenate(taps, axis=0), preferred_element_type=F32)
         back[:, :, :, chans] = total.reshape(2, 14, 16, CG)[:, :, 0:14, :].astype(BF16)
 
     def send(src, dst, send_sem, recv_sem, device):

time: 36.1 us -> 36.1 us (level)
  no operation moved by 1% of the time
where the time goes in v7:
time: 36.1 us; the launch traced here: 36 us
  Pallas kernels  30.6 us (85%)
  local copies, waits for them, and re-layouts  4.01 us (11%)
  between operations  0.73 us (2%)
  other arithmetic  0.68 us (2%)
    pallas_call x1, Pallas kernels, fused_on_device(): pl.pallas_call(step_kernel, out_shape=(jax.ShapeDtypeStruct(activations.s...  30.6 us
    unnamed x14, local copies, waits for them, and re-layouts  4.01 us

profile of v7, /device:TPU:1, one launch (start us, length us, event | category | flops | bytes accessed | tf_op | source)
XLA Modules:
  0.0 36.0 jit_solution(15884414704449553217)
XLA Ops:
  0.6 0.0 copy-start.3
  0.6 1.1 %copy.12.act = bf16[2,14,14,384]{3,2,1,0:T(8,128)(2,1)S(1)} copy(bf16[2,14,14,384]{3,0,2,1:T(2,128)(2,1)} %param.7) | data formatting | bytes 602112 | tf_op args[0]
  1.7 0.0 copy-start
  1.7 0.0 copy-start.1
  1.8 0.0 copy-start.2
  1.8 0.0 copy-start.4
  1.8 1.0 %copy.13.cot = bf16[2,14,14,384]{3,2,1,0:T(8,128)(2,1)S(1)} copy(bf16[2,14,14,384]{3,0,2,1:T(2,128)(2,1)} %param.8) | data formatting | bytes 602112 | tf_op args[1]
  2.8 0.0 copy-done.3
  2.8 0.0 copy-done
  2.8 0.0 copy-done.1
  2.8 0.0 copy-done.2
  2.9 0.0 copy-done.4
  2.9 30.6 %shard_map.110 = (bf16[2,14,14,384]{3,2,1,0:T(8,128)(2,1)S(1)}, f32[108,128]{1,0:T(8,128)S(1)}, bf16[384,1152]{1,0:T(8,128)(2,1)S(1)}) custom-call(bf16[2,14,14,384]{3,2,1,0:T(8,128)(2,1)S(1)} %copy.12.act, bf16[2,14,14,384]{3,2,1,0:T(8,128)(2,1)S(1)} %copy.13.cot, bf16[384,1152]{1,0:T(8,128)(2,1)S(1)} %copy-done.3, f32[3,128]{1,0:T(4,128)S(1)} %bitcast.14, ...), custom_call_target="tpu_custom_call" | custom-call | flops 1100000000 | bytes 4000000 | tf_op jit(solution)/shard_map/pallas_call | solution.py:343
  33.4 0.9 %copy.14 = bf16[2,14,14,384]{3,0,2,1:T(2,128)(2,1)} copy(bf16[2,14,14,384]{3,2,1,0:T(8,128)(2,1)S(1)} %get-tuple-element.11) | data formatting | bytes 602112
  34.4 0.7 %multiply_subtract_fusion = (f32[13824]{0:T(1024)}, f32[13824]{0:T(1024)}, f32[13824]{0:T(1024)}) fusion(f32[13824]{0:T(1024)S(1)} %copy-done, f32[108,128]{1,0:T(8,128)S(1)} %get-tuple-element.9, f32[13824]{0:T(1024)S(1)} %copy-done.1, f32[13824]{0:T(1024)S(1)} %copy-done.2), kind=kLoop, calls=%fused_computation.4 | loop fusion | flops 179712 | bytes 387072 | tf_op jit(solution)/shard_map/sub | solution.py:90
  35.1 0.9 %copy.16 = bf16[384,1152]{1,0:T(8,128)(2,1)} copy(bf16[384,1152]{1,0:T(8,128)(2,1)S(1)} %get-tuple-element.28) | data formatting | bytes 1769472
Async XLA Ops:
  0.6 2.2 %copy-start.3 = (bf16[384,1152]{1,0:T(8,128)(2,1)S(1)}, bf16[384,1152]{1,0:T(8,128)(2,1)}, u32[]{:S(2)}) copy-start(bf16[384,1152]{1,0:T(8,128)(2,1)} %ker.1) | copy-start | bytes 2654212
  1.7 1.1 %copy-start = (f32[13824]{0:T(1024)S(1)}, f32[13824]{0:T(1024)}, u32[]{:S(2)}) copy-start(f32[13824]{0:T(1024)} %param.11) | copy-start | bytes 165892
  1.7 1.1 %copy-start.1 = (f32[13824]{0:T(1024)S(1)}, f32[13824]{0:T(1024)}, u32[]{:S(2)}) copy-start(f32[13824]{0:T(1024)} %param.12) | copy-start | bytes 165892
  1.8 1.1 %copy-start.2 = (f32[13824]{0:T(1024)S(1)}, f32[13824]{0:T(1024)}, u32[]{:S(2)}) copy-start(f32[13824]{0:T(1024)} %param.13) | copy-start | bytes 165892
  1.8 1.1 %copy-start.4 = (f32[384]{0:T(512)S(1)}, f32[384]{0:T(512)}, u32[]{:S(2)}) copy-start(f32[384]{0:T(512)} %param.10) | copy-start | bytes 4612
